TPU v7x, 256 devices: a whole 4x4x8 slice. The times are simulated.
256 devices in a mesh: tiles: 64 (over x, z, core), chan: 4 (over y).
Axes of the slice: x: 4, y: 4, z: 8, core: 2. Of those that a mesh axis runs over, the one named last changes fastest.
Arguments:
- ocean_state: bfloat16 [64, 200, 32, 128], P('tiles', 'chan'), may hold values from -6 to 6
- first_weight: bfloat16 [9, 200, 200], P(None, None, 'chan'), may hold values from -0.125 to 0.125
- first_bias: float32 [200], P('chan'), may hold values from -3 to 3
- second_weight: bfloat16 [9, 200, 200], P(None, None, 'chan'), may hold values from -0.125 to 0.125
- second_bias: float32 [200], P('chan'), may hold values from -3 to 3
- wet_mask: int32 [64, 32, 128], P('tiles'), may hold values from 0 to 1
- neighbours: int32 [64, 8], P('tiles'), may hold values from -1 to 63, as said below
- fold_flags: int32 [64, 8], P('tiles'), may hold values from 0 to 1, as said below
Outputs:
- updated_state: bfloat16 [64, 200, 32, 128], P('tiles', 'chan')
Inputs may be any that keep to these rules, and one draw needn't show every extreme that they name: `neighbours`: entries are patch indices or -1. A patch's N and S entries differ, its E and W entries differ and its four diagonal entries differ, where not -1. The relation is mutual: if q is the direction-k neighbour of p, p is q's neighbour in the opposite direction, or in the same direction where the entry crosses the fold. `fold_flags`: only N, NE and NW entries of patches in the northernmost row of patches may be 1, and only where the neighbour is not -1.
All inputs are finite; a program needn't handle non-finite values.
Results may differ from a plain program's by a relative error of at most 0.0033.
Values may be sent and summed in bfloat16 or wider, within the bound.
A program may use at most 128 MiB of HBM per device.

v0:
```python
import jax
import jax.numpy as jnp
from jax import lax
from jax.sharding import PartitionSpec as P


def conv_total(padded, weight):
    channels = padded.shape[0]
    row_count = padded.shape[1] - 2
    col_count = padded.shape[2] - 2
    windows = []
    for tap_index in range(9):
        row_shift = tap_index // 3
        col_shift = tap_index % 3
        window = padded[:, row_shift : row_shift + row_count, col_shift : col_shift + col_count]
        windows.append(window.reshape(channels, row_count * col_count))
    stacked = jnp.concatenate(windows, axis=0)
    flat_weight = weight.reshape(9 * channels, weight.shape[2])
    return lax.dot_general(
        flat_weight, stacked, (((0,), (0,)), ((), ())), preferred_element_type=jnp.float32
    )


def build_sends(values, neighbour_ids, fold_bits):
    peer_count = lax.axis_size("tiles")
    channels, row_count, col_count = values.shape
    top_row = values[:, row_count - 1, :]
    north_send = jnp.where(fold_bits[0] == 1, top_row[:, ::-1], top_row)

    def target(direction):
        return jnp.where(neighbour_ids[direction] >= 0, neighbour_ids[direction], peer_count)

    vertical = jnp.zeros((peer_count, channels, col_count), values.dtype)
    vertical = vertical.at[target(0)].set(north_send, mode="drop")
    vertical = vertical.at[target(1)].set(values[:, 0, :], mode="drop")
    sideways = jnp.zeros((peer_count, channels, row_count), values.dtype)
    sideways = sideways.at[target(2)].set(values[:, :, col_count - 1], mode="drop")
    sideways = sideways.at[target(3)].set(values[:, :, 0], mode="drop")
    corner_cells = jnp.zeros((peer_count, channels), values.dtype)
    corner_cells = corner_cells.at[target(4)].set(
        values[:, row_count - 1, col_count - 1], mode="drop"
    )
    corner_cells = corner_cells.at[target(5)].set(values[:, row_count - 1, 0], mode="drop")
    corner_cells = corner_cells.at[target(6)].set(values[:, 0, col_count - 1], mode="drop")
    corner_cells = corner_cells.at[target(7)].set(values[:, 0, 0], mode="drop")
    return (vertical, sideways, corner_cells)


def frame_patch(
    values,
    north_strip,
    south_strip,
    east_strip,
    west_strip,
    north_east,
    north_west,
    south_east,
    south_west,
):
    middle = jnp.concatenate([west_strip[:, :, None], values, east_strip[:, :, None]], axis=2)
    south_row = jnp.concatenate([south_west[:, None], south_strip, south_east[:, None]], axis=1)
    north_row = jnp.concatenate([north_west[:, None], north_strip, north_east[:, None]], axis=1)
    return jnp.concatenate([south_row[:, None], middle, north_row[:, None]], axis=1)


def assemble(values, vertical, sideways, corner_cells, neighbour_ids):

    def fetch_strip(buffer, direction):
        source = jnp.maximum(neighbour_ids[direction], 0)
        usable = (neighbour_ids[direction] >= 0).astype(buffer.dtype)
        return buffer[source] * usable

    return frame_patch(
        values,
        fetch_strip(vertical, 0),
        fetch_strip(vertical, 1),
        fetch_strip(sideways, 2),
        fetch_strip(sideways, 3),
        fetch_strip(corner_cells, 4),
        fetch_strip(corner_cells, 5),
        fetch_strip(corner_cells, 6),
        fetch_strip(corner_cells, 7),
    )


def layer_sum(share_values, weight, neighbour_ids, fold_bits):
    complete = lax.all_gather(share_values, "chan", axis=0, tiled=True)
    vertical, sideways, corner_cells = build_sends(complete, neighbour_ids, fold_bits)
    vertical, sideways, corner_cells = (
        lax.all_to_all(vertical, "tiles", split_axis=0, concat_axis=0, tiled=True),
        lax.all_to_all(sideways, "tiles", split_axis=0, concat_axis=0, tiled=True),
        lax.all_to_all(corner_cells, "tiles", split_axis=0, concat_axis=0, tiled=True),
    )
    padded = assemble(complete, vertical, sideways, corner_cells, neighbour_ids)
    return conv_total(padded, weight)


def body(
    ocean_state,
    first_weight,
    first_bias,
    second_weight,
    second_bias,
    wet_mask,
    neighbours,
    fold_flags,
):
    neighbour_ids = neighbours[0]
    fold_bits = fold_flags[0]
    state_share = ocean_state[0]
    share_count, row_count, col_count = state_share.shape
    mask_values = wet_mask[0].astype(jnp.bfloat16)
    mask_flat = wet_mask[0].reshape(1, -1).astype(jnp.float32)
    masked = state_share * mask_values[None]
    first_total = layer_sum(masked, first_weight, neighbour_ids, fold_bits)
    hidden = (mask_flat * jax.nn.gelu(first_total + first_bias[:, None])).astype(jnp.bfloat16)
    hidden = hidden.reshape(share_count, row_count, col_count)
    second_total = layer_sum(hidden, second_weight, neighbour_ids, fold_bits)
    residual = state_share.reshape(share_count, -1).astype(jnp.float32)
    result = mask_flat * (residual + second_total + second_bias[:, None])
    return result.astype(jnp.bfloat16).reshape(1, share_count, row_count, col_count)


def solution(mesh):
    return jax.shard_map(
        body,
        mesh=mesh,
        in_specs=(
            P("tiles", "chan", None, None),
            P(None, None, "chan"),
            P("chan"),
            P(None, None, "chan"),
            P("chan"),
            P("tiles", None, None),
            P("tiles", None),
            P("tiles", None),
        ),
        out_specs=P("tiles", "chan", None, None),
        check_vma=False,
    )
```

profile of v0, /device:TPU:1, one launch (start us, length us, event | category | flops | bytes accessed | tf_op | source)
XLA Modules:
  0.0 450.3 jit_solution(9329229004075384950)
XLA Ops:
  24.3 19.1 %all-gather.3.cloned.1.call-done = bf16[200,32,128]{2,1,0:T(8,128)(2,1)} async-done(((bf16[50,32,128]{2,1,0:T(8,128)(2,1)}), bf16[200,32,128]{2,1,0:T(8,128)(2,1)}) %all-gather.3.cloned.1.call-update) | async-done | bytes 1638416 | tf_op jit(solution)/shard_map/all_gather | solution.py:87
  43.3 4.2 slice_reduce_fusion.3
  50.4 10.7 %all-to-all-start = ((bf16[64,1,200]{2,1,0:T(2,128)(2,1)}), bf16[64,1,200]{2,1,0:T(2,128)(2,1)S(1)}, u32[]{:S(2)}, u32[]{:S(2)}) async-start(bf16[64,1,200]{2,1,0:T(2,128)(2,1)} %copy.255), calls=%async_computation | async-start | bytes 131072 | tf_op jit(solution)/shard_map/all_to_all | solution.py:92
  61.0 3.9 fusion.47
  73.5 10.3 %all-to-all-start.2 = ((bf16[64,200,32]{1,2,0:T(8,128)(2,1)}), bf16[64,200,32]{1,2,0:T(8,128)(2,1)S(1)}, u32[]{:S(2)}, u32[]{:S(2)}) async-start(bf16[64,200,32]{1,2,0:T(8,128)(2,1)} %fusion.21), calls=%async_computation.2 | async-start | bytes 2097152 | tf_op jit(solution)/shard_map/all_to_all | solution.py:91
  89.8 22.6 %all-to-all-done.2 = bf16[64,200,32]{1,2,0:T(8,128)(2,1)S(1)} async-done(((bf16[64,200,32]{1,2,0:T(8,128)(2,1)}), bf16[64,200,32]{1,2,0:T(8,128)(2,1)S(1)}, u32[]{:S(2)}, u32[]{:S(2)}) %all-to-all-start.2) | async-done | bytes 819232 | tf_op jit(solution)/shard_map/all_to_all | solution.py:91
  112.4 6.4 %all-to-all-start.1 = ((bf16[64,200,128]{2,1,0:T(8,128)(2,1)}), bf16[64,200,128]{2,1,0:T(8,128)(2,1)}, u32[]{:S(2)}, u32[]{:S(2)}) async-start(bf16[64,200,128]{2,1,0:T(8,128)(2,1)} %fusion.19), calls=%async_computation.1 | async-start | bytes 6553600 | tf_op jit(solution)/shard_map/all_to_all | solution.py:90
  130.6 3.0 copy.264
  133.6 4.9 %pad_maximum_fusion.4 = (bf16[200,32,128]{2,1,0:T(8,128)(2,1)}, bf16[200,32,128]{2,1,0:T(8,128)(2,1)}) fusion(bf16[200,32,1]{2,1,0:T(8,128)(2,1)} %copy.264, bf16[200,32,128]{2,1,0:T(8,128)(2,1)S(1)} %copy-done, bf16[200,32,1]{2,1,0:T(8,128)(2,1)S(1)} %copy.263), kind=kLoop, calls=%fused_computation.31 | loop fusion | flops 6553600 | bytes 4940800 | tf_op jit(solution)/shard_map/concatenate | solution.py:60
  138.5 56.5 %all-to-all-done.1 = bf16[64,200,128]{2,1,0:T(8,128)(2,1)} async-done(((bf16[64,200,128]{2,1,0:T(8,128)(2,1)}), bf16[64,200,128]{2,1,0:T(8,128)(2,1)}, u32[]{:S(2)}, u32[]{:S(2)}) %all-to-all-start.1) | async-done | bytes 3276832 | tf_op jit(solution)/shard_map/all_to_all | solution.py:90
  197.2 9.3 %pad_maximum_fusion = (bf16[200,33,130]{2,1,0:T(8,128)(2,1)S(1)}, bf16[200,33,130]{2,1,0:T(8,128)(2,1)S(1)}) fusion(bf16[200,1,130]{2,1,0:T(2,128)(2,1)S(1)} %copy.271, bf16[200,32,1]{2,1,0:T(8,128)(2,1)} %copy.264, bf16[200,32,128]{2,1,0:T(8,128)(2,1)S(1)} %copy-done, bf16[200,32,1]{2,1,0:T(8,128)(2,1)S(1)} %copy.263, bf16[200,1,130]{2,1,0:T(2,128)(2,1)S(1)} %copy.265), kind=kLoop, calls=%fused_computation.8 | loop fusion | flops 13728000 | bytes 5200000 | tf_op jit(solution)/shard_map/concatenate | solution.py:63
  227.6 8.4 %fusion.13 = bf16[50,4096]{1,0:T(8,128)(2,1)S(1)} fusion(bf16[1800,4096]{1,0:T(8,128)(2,1)} %bitcast_dynamic-update-slice_fusion.9, bf16[1800,50]{0,1:T(8,128)(2,1)S(1)} %reshape.797, f32[50]{0:T(128)S(1)} %copy-done.18, f32[4096]{0:T(1024)S(1)} %copy-done.13), kind=kOutput, calls=%fused_computation.42 | convolution fusion | flops 739532800 | bytes 15351784 | tf_op jit(solution)/shard_map/dot_general | solution.py:19
  236.9 24.9 %all-gather.5.cloned.1.call-done = bf16[200,32,128]{2,1,0:T(8,128)(2,1)} async-done(((bf16[50,32,128]{2,1,0:T(8,128)(2,1)}), bf16[200,32,128]{2,1,0:T(8,128)(2,1)}) %all-gather.5.cloned.1.call-update) | async-done | bytes 1638416 | tf_op jit(solution)/shard_map/all_gather | solution.py:87
  261.7 3.9 fusion.45
  275.6 10.7 %all-to-all-start.3 = ((bf16[64,1,200]{2,1,0:T(2,128)(2,1)}), bf16[64,1,200]{2,1,0:T(2,128)(2,1)S(1)}, u32[]{:S(2)}, u32[]{:S(2)}) async-start(bf16[64,1,200]{2,1,0:T(2,128)(2,1)} %copy.273), calls=%async_computation.3 | async-start | bytes 131072 | tf_op jit(solution)/shard_map/all_to_all | solution.py:92
  290.5 5.6 %all-to-all-done.3 = bf16[64,1,200]{2,1,0:T(2,128)(2,1)S(1)} async-done(((bf16[64,1,200]{2,1,0:T(2,128)(2,1)}), bf16[64,1,200]{2,1,0:T(2,128)(2,1)S(1)}, u32[]{:S(2)}, u32[]{:S(2)}) %all-to-all-start.3) | async-done | bytes 25632 | tf_op jit(solution)/shard_map/all_to_all | solution.py:92
  296.0 4.8 %all-to-all-start.5 = ((bf16[64,200,32]{1,2,0:T(8,128)(2,1)}), bf16[64,200,32]{1,2,0:T(8,128)(2,1)S(1)}, u32[]{:S(2)}, u32[]{:S(2)}) async-start(bf16[64,200,32]{1,2,0:T(8,128)(2,1)} %fusion.20), calls=%async_computation.5 | async-start | bytes 2097152 | tf_op jit(solution)/shard_map/all_to_all | solution.py:91
  306.7 22.6 %all-to-all-done.5 = bf16[64,200,32]{1,2,0:T(8,128)(2,1)S(1)} async-done(((bf16[64,200,32]{1,2,0:T(8,128)(2,1)}), bf16[64,200,32]{1,2,0:T(8,128)(2,1)S(1)}, u32[]{:S(2)}, u32[]{:S(2)}) %all-to-all-start.5) | async-done | bytes 819232 | tf_op jit(solution)/shard_map/all_to_all | solution.py:91
  329.4 6.7 %all-to-all-start.4 = ((bf16[64,200,128]{2,1,0:T(8,128)(2,1)}), bf16[64,200,128]{2,1,0:T(8,128)(2,1)}, u32[]{:S(2)}, u32[]{:S(2)}) async-start(bf16[64,200,128]{2,1,0:T(8,128)(2,1)} %fusion.17), calls=%async_computation.4 | async-start | bytes 6553600 | tf_op jit(solution)/shard_map/all_to_all | solution.py:90
  343.5 3.0 copy.282
  346.5 4.9 %pad_maximum_fusion.2 = (bf16[200,32,128]{2,1,0:T(8,128)(2,1)}, bf16[200,32,128]{2,1,0:T(8,128)(2,1)}) fusion(bf16[200,32,1]{2,1,0:T(8,128)(2,1)} %copy.282, bf16[200,32,128]{2,1,0:T(8,128)(2,1)S(1)} %copy-done.1, bf16[200,32,1]{2,1,0:T(8,128)(2,1)S(1)} %copy.281), kind=kLoop, calls=%fused_computation.29 | loop fusion | flops 6553600 | bytes 4940800 | tf_op jit(solution)/shard_map/concatenate | solution.py:60
  351.4 60.7 %all-to-all-done.4 = bf16[64,200,128]{2,1,0:T(8,128)(2,1)} async-done(((bf16[64,200,128]{2,1,0:T(8,128)(2,1)}), bf16[64,200,128]{2,1,0:T(8,128)(2,1)}, u32[]{:S(2)}, u32[]{:S(2)}) %all-to-all-start.4) | async-done | bytes 3276832 | tf_op jit(solution)/shard_map/all_to_all | solution.py:90
  415.2 9.0 %pad_maximum_fusion.1 = (bf16[200,33,130]{2,1,0:T(8,128)(2,1)S(1)}, bf16[200,33,130]{2,1,0:T(8,128)(2,1)S(1)}) fusion(bf16[200,1,130]{2,1,0:T(2,128)(2,1)S(1)} %copy.289, bf16[200,32,1]{2,1,0:T(8,128)(2,1)} %copy.282, bf16[200,32,128]{2,1,0:T(8,128)(2,1)S(1)} %copy-done.1, bf16[200,32,1]{2,1,0:T(8,128)(2,1)S(1)} %copy.281, bf16[200,1,130]{2,1,0:T(2,128)(2,1)S(1)} %copy.283), kind=kLoop, calls=%fused_computation.10 | loop fusion | flops 13728000 | bytes 5200000 | tf_op jit(solution)/shard_map/concatenate | solution.py:63
  427.8 4.1 fusion.40
  (147 shorter events, 100.8 us)
Async XLA Ops:
  6.5 36.8 %all-gather.3.cloned.1.call-start = ((), (), s32[]{:S(2)}) async-start(), calls=%async_computation.6 | async-start | bytes 2048000 | tf_op jit(solution)/shard_map/all_gather | solution.py:87
  50.4 23.2 %all-to-all-start = ((bf16[64,1,200]{2,1,0:T(2,128)(2,1)}), bf16[64,1,200]{2,1,0:T(2,128)(2,1)S(1)}, u32[]{:S(2)}, u32[]{:S(2)}) async-start(bf16[64,1,200]{2,1,0:T(2,128)(2,1)} %copy.255), calls=%async_computation | async-start | bytes 131072 | tf_op jit(solution)/shard_map/all_to_all | solution.py:92
  65.0 18.9 %copy-start.17 = (s32[1,8]{1,0:T(1,128)S(1)}, s32[1,8]{1,0:T(1,128)}, u32[]{:S(2)}) copy-start(s32[1,8]{1,0:T(1,128)} %param.47) | copy-start | bytes 100
  65.0 18.9 %copy-start = (bf16[200,32,128]{2,1,0:T(8,128)(2,1)S(1)}, bf16[200,32,128]{2,1,0:T(8,128)(2,1)}, u32[]{:S(2)}) copy-start(bf16[200,32,128]{2,1,0:T(8,128)(2,1)} %all-gather.3.cloned.1.call-done) | copy-start | bytes 4915204
  73.5 14.3 %copy-start.15 = (bf16[64,1,200]{2,1,0:T(2,128)(2,1)}, bf16[64,1,200]{2,1,0:T(2,128)(2,1)S(1)}, u32[]{:S(2)}) copy-start(bf16[64,1,200]{2,1,0:T(2,128)(2,1)S(1)} %all-to-all-done) | copy-start | bytes 76804
  73.5 38.9 %all-to-all-start.2 = ((bf16[64,200,32]{1,2,0:T(8,128)(2,1)}), bf16[64,200,32]{1,2,0:T(8,128)(2,1)S(1)}, u32[]{:S(2)}, u32[]{:S(2)}) async-start(bf16[64,200,32]{1,2,0:T(8,128)(2,1)} %fusion.21), calls=%async_computation.2 | async-start | bytes 2097152 | tf_op jit(solution)/shard_map/all_to_all | solution.py:91
  89.8 34.2 %copy-start.11 = (bf16[9,200,50]{1,2,0:T(8,128)(2,1)S(1)}, bf16[9,200,50]{1,2,0:T(8,128)(2,1)}, u32[]{:S(2)}) copy-start(bf16[9,200,50]{1,2,0:T(8,128)(2,1)} %param.41) | copy-start | bytes 540004
  112.4 82.6 %all-to-all-start.1 = ((bf16[64,200,128]{2,1,0:T(8,128)(2,1)}), bf16[64,200,128]{2,1,0:T(8,128)(2,1)}, u32[]{:S(2)}, u32[]{:S(2)}) async-start(bf16[64,200,128]{2,1,0:T(8,128)(2,1)} %fusion.19), calls=%async_computation.1 | async-start | bytes 6553600 | tf_op jit(solution)/shard_map/all_to_all | solution.py:90
  118.8 142.9 %all-gather.5.cloned.1.call-start = ((), (), s32[]{:S(2)}) async-start(), calls=%async_computation.7 | async-start | bytes 2048000 | tf_op jit(solution)/shard_map/all_gather | solution.py:87
  212.5 3.8 copy-start.8
  216.2 3.8 copy-start.6
  223.8 3.8 copy-start.13
  223.8 3.8 copy-start.18
  265.7 4.3 copy-start.1
  275.6 20.5 %all-to-all-start.3 = ((bf16[64,1,200]{2,1,0:T(2,128)(2,1)}), bf16[64,1,200]{2,1,0:T(2,128)(2,1)S(1)}, u32[]{:S(2)}, u32[]{:S(2)}) async-start(bf16[64,1,200]{2,1,0:T(2,128)(2,1)} %copy.273), calls=%async_computation.3 | async-start | bytes 131072 | tf_op jit(solution)/shard_map/all_to_all | solution.py:92
  296.0 33.3 %all-to-all-start.5 = ((bf16[64,200,32]{1,2,0:T(8,128)(2,1)}), bf16[64,200,32]{1,2,0:T(8,128)(2,1)S(1)}, u32[]{:S(2)}, u32[]{:S(2)}) async-start(bf16[64,200,32]{1,2,0:T(8,128)(2,1)} %fusion.20), calls=%async_computation.5 | async-start | bytes 2097152 | tf_op jit(solution)/shard_map/all_to_all | solution.py:91
  306.7 29.4 %copy-start.10 = (bf16[1,50,32,128]{3,2,1,0:T(8,128)(2,1)S(1)}, bf16[1,50,32,128]{3,2,1,0:T(8,128)(2,1)}, u32[]{:S(2)}) copy-start(bf16[1,50,32,128]{3,2,1,0:T(8,128)(2,1)} %param.40) | copy-start | bytes 1228804
  329.4 82.8 %all-to-all-start.4 = ((bf16[64,200,128]{2,1,0:T(8,128)(2,1)}), bf16[64,200,128]{2,1,0:T(8,128)(2,1)}, u32[]{:S(2)}, u32[]{:S(2)}) async-start(bf16[64,200,128]{2,1,0:T(8,128)(2,1)} %fusion.17), calls=%async_computation.4 | async-start | bytes 6553600 | tf_op jit(solution)/shard_map/all_to_all | solution.py:90
  336.1 1.7 copy-start.12
  431.9 2.3 copy-start.4
  431.9 3.0 copy-start.7
  435.6 1.6 copy-start.3
  436.4 1.6 copy-start.2
  437.9 1.4 copy-start.16
  (3 other events, 4.3 us)
Sparse Core Ops, SparseCore 0:
  9.9 33.4 all-gather.2
  237.0 24.6 all-gather.4
where the time goes:
time: 459 us; the launch traced here: 450 us
  waiting for transfers between devices  212 us (46%)
  local copies, waits for them, and re-layouts  83.5 us (18%)
  other arithmetic  64.4 us (14%)
  starting transfers between devices  49.8 us (11%)
  between operations  29.5 us (6%)
  matrix products  11.2 us (2%)
    all_to_all x2, waiting for transfers between devices, layer_sum(): lax.all_to_all(vertical, 'tiles', split_axis=0, concat_axis=0, tiled=True)  117 us
    all_to_all x2, waiting for transfers between devices, layer_sum(): lax.all_to_all(sideways, 'tiles', split_axis=0, concat_axis=0, tiled=True)  45.2 us
    all_gather x2, waiting for transfers between devices, layer_sum(): complete = lax.all_gather(share_values, 'chan', axis=0, tiled=True)  43.9 us
    unnamed x66, local copies, waits for them, and re-layouts  33 us
    all_to_all x2, starting transfers between devices, layer_sum(): lax.all_to_all(corner_cells, 'tiles', split_axis=0, concat_axis=0, tiled=...  21.3 us
    concatenate x2, other arithmetic, frame_patch(): jnp.concatenate([south_row[:, None], middle, north_row[:, None]], axis=1)  18.3 us
    mul x12, local copies, waits for them, and re-layouts, fetch_strip(): return buffer[source] * usable  15.2 us
    all_to_all x2, starting transfers between devices, layer_sum(): lax.all_to_all(sideways, 'tiles', split_axis=0, concat_axis=0, tiled=True)  15.1 us
  transfers between devices with their start and end apart: 8, of which 7 were waited for; matrix products, arithmetic and copies ran while one was open for 14% of the time, Pallas kernels for 0%

commit v1 on v0

v1 whole, which is shorter than its diff:
```python
import functools
import math

import jax
import jax.numpy as jnp
from jax import lax
from jax.experimental import pallas as pl
from jax.experimental.pallas import tpu as pltpu
from jax.sharding import PartitionSpec as P

MESH = pl.DeviceIdType.MESH
LANES = 128
SLOT = 64
PEERS = 4
X_SIZE = 4
Z_SIZE = 8


def body_kernel(
    geo,
    state,
    w1,
    b1,
    w2,
    b2,
    wet,
    nb,
    fold,
    out,
    flat,
    share,
    packed,
    packed_halo,
    taps_f,
    taps,
    rows_z,
    sums,
    ring,
    ring_z0,
    ring_z1,
    slots,
    slots_x0,
    slots_x1,
    halo,
    table_own,
    table,
    table_s,
    y_send,
    y_recv,
    h_send,
    h_recv,
    z_send,
    z_recv,
    u_send,
    u_recv,
    t_send,
    t_recv,
    local_sem,
):
    xs, zs, ch, chp, nr = geo
    us = 2 * xs
    ring_z, slots_x = (ring_z0, ring_z1), (slots_x0, slots_x1)
    pairs = nr // 2
    half = pairs // 2
    f32, bf16 = jnp.float32, jnp.bfloat16

    t = lax.axis_index("tiles")
    c = lax.axis_index("chan")
    k = lax.rem(t, 2)
    z = lax.rem(t // 2, zs)
    x = t // (2 * zs)
    u = x * 2 + k
    up = lax.rem(c + 1, PEERS)
    down = lax.rem(c + PEERS - 1, PEERS)

    def z_peer(o):
        return (x * zs + lax.rem(z + o, zs)) * 2 + k

    def u_peer(o):
        v = lax.rem(u + o, us)
        return ((v // 2) * zs + z) * 2 + lax.rem(v, 2)

    lane = lax.broadcasted_iota(jnp.int32, (chp, LANES), 1)

    barrier = pltpu.get_barrier_semaphore()
    for o in range(1, PEERS):
        pl.semaphore_signal(barrier, inc=1, device_id=(t, lax.rem(c + o, PEERS)), device_id_type=MESH)
    for o in range(1, zs):
        pl.semaphore_signal(barrier, inc=1, device_id=(z_peer(o), c), device_id_type=MESH)
    for o in range(1, us):
        pl.semaphore_signal(barrier, inc=1, device_id=(u_peer(o), c), device_id_type=MESH)

    flat[0 : ch * nr] = state[0].astype(f32).reshape(ch * nr, LANES)
    flat[ch * nr : chp * nr] = jnp.zeros(((chp - ch) * nr, LANES), f32)

    def put_row(layer, i, h, row, sides):
        r = 2 * i + h
        row16 = row.astype(bf16)
        share[layer, 0, i, :, h * LANES : (h + 1) * LANES] = row16
        sides = jnp.where(lane == 1 + r, pltpu.roll(row, r + 2, 1), sides)
        return jnp.where(lane == 65 + r, pltpu.roll(row, r + 65, 1), sides)

    def mask_row(r):
        return wet[0, pl.ds(r, 1), :].astype(f32)

    def load_pair(i, sides):
        for h in range(2):
            r = 2 * i + h
            row = flat[pl.ds(r, chp, stride=nr), :] * mask_row(r)
            sides = put_row(0, i, h, row, sides)
        return sides

    def put_ring(layer, sides):
        ring[layer, :, 0:LANES] = share[layer, 0, 0, :, 0:LANES]
        ring[layer, :, LANES : 2 * LANES] = share[layer, 0, pairs - 1, :, LANES : 2 * LANES]
        ring[layer, :, 2 * LANES : 3 * LANES] = sides.astype(bf16)

    put_ring(0, lax.fori_loop(0, pairs, load_pair, jnp.zeros((chp, LANES), f32)))
    table_own[...] = jnp.zeros((8, LANES), jnp.int32)
    table_own[0:1, 0:8] = nb[...] * 2 + fold[...]

    pl.semaphore_wait(barrier, (PEERS - 1) + (zs - 1) + (us - 1))

    def remote(src, dst, send, recv, tile, chan):
        return pltpu.make_async_remote_copy(
            src_ref=src, dst_ref=dst, send_sem=send, recv_sem=recv, device_id=(tile, chan), device_id_type=MESH
        )

    first, second = pl.ds(0, half), pl.ds(half, half)

    def y_copy(layer, n):
        src, dst, part, chan = (
            (0, 3, first, up),
            (0, 3, second, up),
            (0, 1, second, down),
            (0, 1, first, down),
            (3, 2, first, up),
            (1, 2, second, down),
        )[n]
        return remote(
            share.at[layer, src, part], share.at[layer, dst, part], y_send.at[layer, n], y_recv.at[layer, n], t, chan
        )

    def z_copy(layer, o):
        return remote(ring.at[layer], ring_z[layer].at[z], z_send.at[layer, o], z_recv.at[layer, o], z_peer(o), c)

    def u_copy(layer, o):
        return remote(
            slots.at[layer, lax.rem(u + o, us)],
            slots_x[layer].at[u],
            u_send.at[layer, o],
            u_recv.at[layer, o],
            u_peer(o),
            c,
        )

    def t_copy(o):
        return remote(table_own, table.at[u], t_send.at[o], t_recv.at[o], u_peer(o), c)

    def h_copy(layer, o):
        return remote(
            halo.at[layer, 0],
            halo.at[layer, PEERS - o],
            h_send.at[layer, o],
            h_recv.at[layer, o],
            t,
            lax.rem(c + o, PEERS),
        )

    def start_layer(layer):
        for o in range(1, zs):
            z_copy(layer, o).start()
        for n in (0, 2, 1, 3):
            y_copy(layer, n).start()

    start_layer(0)
    for o in range(1, us):
        t_copy(o).start()

    k_in = lax.broadcasted_iota(jnp.int32, (PEERS * ch, PEERS * SLOT), 0)
    k_at = lax.broadcasted_iota(jnp.int32, (PEERS * ch, PEERS * SLOT), 1)
    place = jnp.zeros((PEERS * ch, PEERS * SLOT), jnp.bool_)
    for j in range(PEERS):
        owner = lax.rem(c + j, PEERS)
        place = place | (
            (k_at - SLOT * j == k_in - ch * owner) & (k_at >= SLOT * j) & (k_at < SLOT * j + ch)
        )
    place = jnp.where(place, 1.0, 0.0).astype(bf16)
    taps_f[...] = jnp.zeros(taps_f.shape, f32)
    for layer, w in enumerate((w1, w2)):
        for tap in range(9):
            taps_f[tap * chp : tap * chp + ch, :] = lax.dot_general(
                w[tap], place, (((0,), (0,)), ((), ())), preferred_element_type=f32
            )
        taps[layer] = taps_f[...].astype(bf16)
    packed[...] = jnp.zeros(packed.shape, bf16)
    packed_halo[...] = jnp.zeros(packed_halo.shape, bf16)

    eye = lax.broadcasted_iota(jnp.int32, (chp, ch), 0) == lax.broadcasted_iota(jnp.int32, (chp, ch), 1)

    def bias_column(b):
        spread = jnp.broadcast_to(b[...], (chp, ch))
        return jnp.sum(jnp.where(eye, spread, 0.0), axis=1, keepdims=True)

    flip = jnp.where(
        lax.broadcasted_iota(jnp.int32, (LANES, LANES), 0) + lax.broadcasted_iota(jnp.int32, (LANES, LANES), 1)
        == LANES - 1,
        1.0,
        0.0,
    ).astype(bf16)

    table[u] = table_own[...]
    for o in range(1, us):
        t_copy(o).wait_recv()
    move = pltpu.make_async_copy(table, table_s, local_sem)
    move.start()
    move.wait()

    east, west = (lane >= 65) & (lane < 65 + nr), (lane >= 1) & (lane < 1 + nr)
    sides_at = slice(2 * LANES, 3 * LANES)

    def read_table(v):
        codes = [table_s[v, 0, n] for n in range(8)]
        return [code >> 1 for code in codes], [code & 1 for code in codes]

    def build_slot(layer, v):
        ids, folds = read_table(v)
        at = [lax.rem(jnp.maximum(q, 0) // 2, zs) for q in ids]
        slots[layer, v, :, 0:LANES] = ring_z[layer][at[1], :, LANES : 2 * LANES]
        plain = ring_z[layer][at[0], :, 0:LANES]
        folded = ring_z[layer][at[0], :, LANES : 2 * LANES]
        slots[layer, v, :, LANES : 2 * LANES] = jnp.where(folds[0] == 1, folded, plain)

        def sides(n):
            return ring_z[layer][at[n], :, sides_at].astype(f32)

        result = jnp.where(east, sides(2), sides(3))
        result = jnp.where(lane == 65 + nr, corner_top(sides(4), folds[4]), result)
        result = jnp.where(lane == 1 + nr, corner_top(sides(5), folds[5]), result)
        result = jnp.where(lane == 64, pltpu.roll(sides(6), LANES - nr, 1), result)
        result = jnp.where(lane == 0, pltpu.roll(sides(7), LANES - nr, 1), result)
        slots[layer, v, :, sides_at] = result.astype(bf16)

    def corner_top(v, is_fold):
        return jnp.where(is_fold == 1, pltpu.roll(v, 65, 1), pltpu.roll(v, nr, 1))

    def merge(layer):
        ids, folds = read_table(u)
        at = [(jnp.maximum(q, 0) // (2 * zs)) * 2 + lax.rem(jnp.maximum(q, 0), 2) for q in ids]

        def usable(n, value):
            return jnp.where(ids[n] >= 0, value, jnp.zeros_like(value))

        halo[layer, 0, :, 0:LANES] = usable(1, slots_x[layer][at[1], :, 0:LANES])
        north = slots_x[layer][at[0], :, LANES : 2 * LANES]
        turned = jnp.dot(north, flip, preferred_element_type=f32).astype(bf16)
        halo[layer, 0, :, LANES : 2 * LANES] = usable(0, jnp.where(folds[0] == 1, turned, north))

        def sides(n):
            return usable(n, slots_x[layer][at[n], :, sides_at].astype(f32))

        result = jnp.where(east, sides(2), 0.0)
        result = jnp.where(west, sides(3), result)
        result = jnp.where(lane == 65 + nr, sides(4), result)
        result = jnp.where(lane == 1 + nr, sides(5), result)
        result = jnp.where(lane == 64, sides(6), result)
        result = jnp.where(lane == 0, sides(7), result)
        halo[layer, 0, :, sides_at] = result.astype(bf16)

    def exchange(layer):
        y_copy(layer, 0).wait_recv()
        y_copy(layer, 4).start()
        y_copy(layer, 2).wait_recv()
        y_copy(layer, 5).start()
        ring_z[layer][z] = ring[layer]
        for o in range(1, zs):
            z_copy(layer, o).wait_recv()

        def one_slot(v, carry):
            build_slot(layer, v)
            return carry

        lax.fori_loop(0, us, one_slot, 0)
        for o in range(1, us):
            u_copy(layer, o).start()
        slots_x[layer][u] = slots[layer, u]
        for o in range(1, us):
            u_copy(layer, o).wait_recv()
        merge(layer)
        for o in range(1, PEERS):
            h_copy(layer, o).start()

    def tap_rows(tap):
        return slice(tap * chp, (tap + 1) * chp)

    def row_sum(r):
        total = []
        for b in range(3):
            total.append(
                rows_z[r, tap_rows(b), :] + rows_z[r + 1, tap_rows(3 + b), :] + rows_z[r + 2, tap_rows(6 + b), :]
            )
        left = jnp.where(lane == 0, 0.0, pltpu.roll(total[0], 1, 1))
        right = jnp.where(lane == LANES - 1, 0.0, pltpu.roll(total[2], LANES - 1, 1))
        return total[1] + left + right

    def conv(layer):
        for n in (1, 3, 4, 5):
            y_copy(layer, n).wait_recv()

        def one_pair(i, carry):
            for j in range(PEERS):
                packed[i, j * SLOT : j * SLOT + chp, :] = share[layer, j, i]
            both = jnp.dot(taps[layer], packed[i], preferred_element_type=f32)
            rows_z[2 * i + 1] = both[:, 0:LANES]
            rows_z[2 * i + 2] = both[:, LANES : 2 * LANES]
            return carry

        lax.fori_loop(0, pairs, one_pair, 0)

        def inner_row(r, carry):
            sums[r] = row_sum(r)
            return carry

        lax.fori_loop(1, nr - 1, inner_row, 0)
        for o in range(1, PEERS):
            h_copy(layer, o).wait_recv()
        for j in range(PEERS):
            packed_halo[j * SLOT : j * SLOT + chp, :] = halo[layer, j]
        frame = jnp.dot(taps[layer], packed_halo[...], preferred_element_type=f32)
        rows_z[0] = frame[:, 0:LANES]
        rows_z[nr + 1] = frame[:, LANES : 2 * LANES]
        sums[0] = row_sum(0)
        sums[nr - 1] = row_sum(nr - 1)
        side = frame[:, sides_at]
        to_west = pltpu.roll(side[tap_rows(0)], 1, 1) + side[tap_rows(3)] + pltpu.roll(side[tap_rows(6)], LANES - 1, 1)
        to_east = pltpu.roll(side[tap_rows(2)], 1, 1) + side[tap_rows(5)] + pltpu.roll(side[tap_rows(8)], LANES - 1, 1)
        return to_west, to_east

    def full_row(r, to_west, to_east):
        edge = jnp.where(lane == 0, pltpu.roll(to_west, LANES - 1 - r, 1), 0.0)
        edge = jnp.where(lane == LANES - 1, pltpu.roll(to_east, 62 - r, 1), edge)
        return sums[r] + edge

    exchange(0)
    to_west, to_east = conv(0)
    bias = bias_column(b1)

    def hidden_pair(i, sides):
        for h in range(2):
            r = 2 * i + h
            v = full_row(r, to_west, to_east) + bias
            v = 0.5 * v * (1.0 + jnp.tanh(math.sqrt(2.0 / math.pi) * (v + 0.044715 * (v * v * v))))
            sides = put_row(1, i, h, v * mask_row(r), sides)
        return sides

    put_ring(1, lax.fori_loop(0, pairs, hidden_pair, jnp.zeros((chp, LANES), f32)))
    start_layer(1)

    exchange(1)
    to_west, to_east = conv(1)
    bias = bias_column(b2)

    def final_pair(i, carry):
        for h in range(2):
            r = 2 * i + h
            own = share[0, 0, i, :, h * LANES : (h + 1) * LANES].astype(f32)
            v = own + full_row(r, to_west, to_east) + bias
            flat[pl.ds(r, chp, stride=nr), :] = v * mask_row(r)
        return carry

    lax.fori_loop(0, pairs, final_pair, 0)
    out[0] = flat[0 : ch * nr].reshape(ch, nr, LANES).astype(bf16)

    for o in range(1, us):
        t_copy(o).wait_send()
    for layer in range(2):
        for n in range(6):
            y_copy(layer, n).wait_send()
        for o in range(1, zs):
            z_copy(layer, o).wait_send()
        for o in range(1, us):
            u_copy(layer, o).wait_send()
        for o in range(1, PEERS):
            h_copy(layer, o).wait_send()


def build(mesh, xs, zs):
    us = 2 * xs

    def body(state, w1, b1, w2, b2, wet, nb, fold):
        ch, nr = state.shape[1], state.shape[2]
        chp = -(-ch // 8) * 8
        pairs = nr // 2
        f32, bf16 = jnp.float32, jnp.bfloat16
        vmem, dma = pltpu.VMEM, pltpu.SemaphoreType.DMA
        inside = pl.BlockSpec(memory_space=pltpu.VMEM)
        return pl.pallas_call(
            functools.partial(body_kernel, (xs, zs, ch, chp, nr)),
            out_shape=jax.ShapeDtypeStruct(state.shape, bf16),
            in_specs=[inside] * 8,
            out_specs=inside,
            scratch_shapes=[
                vmem((chp * nr, LANES), f32),
                vmem((2, PEERS, pairs, chp, 2 * LANES), bf16),
                vmem((pairs, PEERS * SLOT, 2 * LANES), bf16),
                vmem((PEERS * SLOT, 3 * LANES), bf16),
                vmem((9 * chp, PEERS * SLOT), f32),
                vmem((2, 9 * chp, PEERS * SLOT), bf16),
                vmem((nr + 2, 9 * chp, LANES), f32),
                vmem((nr, chp, LANES), f32),
                vmem((2, chp, 3 * LANES), bf16),
                vmem((zs, chp, 3 * LANES), bf16),
                vmem((zs, chp, 3 * LANES), bf16),
                vmem((2, us, chp, 3 * LANES), bf16),
                vmem((us, chp, 3 * LANES), bf16),
                vmem((us, chp, 3 * LANES), bf16),
                vmem((2, PEERS, chp, 3 * LANES), bf16),
                vmem((8, LANES), jnp.int32),
                vmem((us, 8, LANES), jnp.int32),
                pltpu.SMEM((us, 8, LANES), jnp.int32),
                dma((2, 6)),
                dma((2, 6)),
                dma((2, PEERS)),
                dma((2, PEERS)),
                dma((2, zs)),
                dma((2, zs)),
                dma((2, us)),
                dma((2, us)),
                dma((us,)),
                dma((us,)),
                dma,
            ],
            compiler_params=pltpu.CompilerParams(
                collective_id=0, has_side_effects=True, vmem_limit_bytes=48 * 1024 * 1024
            ),
        )(state, w1, b1.reshape(1, -1), w2, b2.reshape(1, -1), wet, nb, fold)

    return jax.shard_map(
        body,
        mesh=mesh,
        in_specs=(
            P("tiles", "chan", None, None),
            P(None, None, "chan"),
            P("chan"),
            P(None, None, "chan"),
            P("chan"),
            P("tiles", None, None),
            P("tiles", None),
            P("tiles", None),
        ),
        out_specs=P("tiles", "chan", None, None),
        check_vma=False,
    )


def solution(mesh):
    return build(mesh, X_SIZE, Z_SIZE)
```

time: 459 us -> 66.8 us (0.15); the launches traced: 450 us -> 66.7 us
  waiting for transfers between devices: 212 us -> 0 us
  local copies, waits for them, and re-layouts: 83.5 us -> 3.03 us
  other arithmetic: 64.4 us -> 0 us
  Pallas kernels: 0 us -> 63.6 us
  starting transfers between devices: 49.8 us -> 0 us
  between operations: 29.5 us -> 0.08 us
  matrix products: 11.2 us -> 0 us
    all_to_all x6 -> x0, waiting for transfers between devices: 168 us -> none  [the longest x2 117 us: layer_sum(): lax.all_to_all(vertical, 'tiles', split_axis=0, concat_axis=0, tiled=True)]
    pallas_call x0 -> x1, Pallas kernels: none -> 63.6 us  [body(): pl.pallas_call(functools.partial(body_kernel, (xs, zs, ch, chp, nr)), out...]
    all_to_all x6 -> x0, starting transfers between devices: 49.5 us -> none  [the longest x2 21.3 us: layer_sum(): lax.all_to_all(corner_cells, 'tiles', split_axis=0, concat_axis=0, tiled=...]
    all_gather x2 -> x0, waiting for transfers between devices: 43.9 us -> none  [layer_sum(): complete = lax.all_gather(share_values, 'chan', axis=0, tiled=True)]
    unnamed x66 -> x17, local copies, waits for them, and re-layouts: 33 us -> 3.03 us
    concatenate x4 -> x0, other arithmetic: 28.1 us -> none  [the longest x2 18.3 us: frame_patch(): jnp.concatenate([south_row[:, None], middle, north_row[:, None]], axis=1)]
    slice x9 -> x0, local copies, waits for them, and re-layouts: 20.9 us -> none  [the longest x4 11 us: conv_total(): padded[:, row_shift:row_shift + row_count, col_shift:col_shift + col_count]]
    mul x12 -> x0, local copies, waits for them, and re-layouts: 15.2 us -> none  [fetch_strip(): return buffer[source] * usable]
  transfers between devices with their start and end apart: 8 -> 0, of which waited for: 7 -> 0; matrix products, arithmetic and copies ran while one was open for 14% -> 0% of each run, Pallas kernels for 0% -> 0%
where the time goes in v1:
time: 66.8 us; the launch traced here: 66.7 us
  Pallas kernels  63.6 us (95%)
  local copies, waits for them, and re-layouts  3.03 us (5%)
    pallas_call x1, Pallas kernels, body(): pl.pallas_call(functools.partial(body_kernel, (xs, zs, ch, chp, nr)), out...  63.6 us
    unnamed x17, local copies, waits for them, and re-layouts  3.03 us

profile of v1, /device:TPU:1, one launch (start us, length us, event | category | flops | bytes accessed | tf_op | source)
XLA Modules:
  0.0 66.7 jit_solution(17116870070555809218)
XLA Ops:
  0.0 0.0 copy-start.6
  0.0 1.3 %copy.9.w1 = bf16[9,200,50]{2,1,0:T(8,128)(2,1)S(1)} copy(bf16[9,200,50]{1,2,0:T(8,128)(2,1)} %param.9) | data formatting | bytes 360000 | tf_op args[1]
  1.3 0.0 copy-done.6
  1.3 0.0 copy-start
  1.3 0.0 copy-start.1
  1.3 0.0 copy-start.2
  1.3 0.0 copy-start.3
  1.4 0.0 copy-start.4
  1.4 0.0 copy-start.5
  1.4 0.3 copy.10.w2
  1.7 0.6 copy-done
  2.3 0.0 copy-done.1
  2.3 0.0 copy-done.2
  2.3 0.0 copy-done.3
  2.3 0.0 copy-done.4
  2.3 0.0 copy-done.5
  2.3 63.6 %shard_map.82 = bf16[1,50,32,128]{3,2,1,0:T(8,128)(2,1)S(1)} custom-call(bf16[1,50,32,128]{3,2,1,0:T(8,128)(2,1)S(1)} %copy-done, bf16[9,200,50]{2,1,0:T(8,128)(2,1)S(1)} %copy.9.w1, f32[1,50]{1,0:T(1,128)S(1)} %bitcast.2, bf16[9,200,50]{2,1,0:T(8,128)(2,1)S(1)} %copy.10.w2, f32[1,50]{1,0:T(1,128)S(1)} %bitcast.3, s32[1,32,128]{2,1,0:T(8,128)S(1)} %copy-done.1, ...), custom_call_target="tpu_custom_call" | custom-call | tf_op jit(solution)/shard_map/pallas_call | solution.py:397
  66.0 0.8 %copy.12 = bf16[1,50,32,128]{3,2,1,0:T(8,128)(2,1)} copy(bf16[1,50,32,128]{3,2,1,0:T(8,128)(2,1)S(1)} %shard_map.82) | data formatting | bytes 819200
Async XLA Ops:
  0.0 1.3 %copy-start.6 = (bf16[9,200,50]{1,2,0:T(8,128)(2,1)S(1)}, bf16[9,200,50]{1,2,0:T(8,128)(2,1)}, u32[]{:S(2)}) copy-start(bf16[9,200,50]{1,2,0:T(8,128)(2,1)} %param.11) | copy-start | bytes 540004
  1.3 1.0 %copy-start = (bf16[1,50,32,128]{3,2,1,0:T(8,128)(2,1)S(1)}, bf16[1,50,32,128]{3,2,1,0:T(8,128)(2,1)}, u32[]{:S(2)}) copy-start(bf16[1,50,32,128]{3,2,1,0:T(8,128)(2,1)} %state.1) | copy-start | bytes 1228804
  1.3 1.0 %copy-start.1 = (s32[1,32,128]{2,1,0:T(8,128)S(1)}, s32[1,32,128]{2,1,0:T(8,128)}, u32[]{:S(2)}) copy-start(s32[1,32,128]{2,1,0:T(8,128)} %wet.1) | copy-start | bytes 49156
  1.3 1.0 %copy-start.2 = (f32[50]{0:T(128)S(1)}, f32[50]{0:T(128)}, u32[]{:S(2)}) copy-start(f32[50]{0:T(128)} %param.10) | copy-start | bytes 604
  1.3 1.0 %copy-start.3 = (f32[50]{0:T(128)S(1)}, f32[50]{0:T(128)}, u32[]{:S(2)}) copy-start(f32[50]{0:T(128)} %param.12) | copy-start | bytes 604
  1.4 1.0 %copy-start.4 = (s32[1,8]{1,0:T(1,128)S(1)}, s32[1,8]{1,0:T(1,128)}, u32[]{:S(2)}) copy-start(s32[1,8]{1,0:T(1,128)} %nb.1) | copy-start | bytes 100
  1.4 1.0 %copy-start.5 = (s32[1,8]{1,0:T(1,128)S(1)}, s32[1,8]{1,0:T(1,128)}, u32[]{:S(2)}) copy-start(s32[1,8]{1,0:T(1,128)} %fold.1) | copy-start | bytes 100

commit v2 on v1

v2 whole, which is shorter than its diff:
```python
import functools
import math

import jax
import jax.numpy as jnp
from jax import lax
from jax.experimental import pallas as pl
from jax.experimental.pallas import tpu as pltpu
from jax.sharding import PartitionSpec as P

MESH = pl.DeviceIdType.MESH
LANES = 128
SLOT = 64
PEERS = 4
X_SIZE = 4
Z_SIZE = 8
CHUNKS = 4


def body_kernel(
    geo,
    state,
    w1,
    b1,
    w2,
    b2,
    wet,
    nb,
    fold,
    out,
    flat,
    share,
    grid,
    sides_k,
    taps_f,
    taps,
    sums,
    ring,
    ring_z0,
    ring_z1,
    slots,
    slots_x0,
    slots_x1,
    halo,
    table_own,
    table,
    table_s,
    y_send,
    y_recv,
    h_send,
    h_recv,
    z_send,
    z_recv,
    u_send,
    u_recv,
    t_send,
    t_recv,
    local_sem,
):
    xs, zs, ch, chp, nr = geo
    us = 2 * xs
    ring_z, slots_x = (ring_z0, ring_z1), (slots_x0, slots_x1)
    pairs = nr // 2
    part = pairs // CHUNKS
    rows_of = 2 * part
    depth = PEERS * SLOT
    f32, bf16 = jnp.float32, jnp.bfloat16

    t = lax.axis_index("tiles")
    c = lax.axis_index("chan")
    k = lax.rem(t, 2)
    z = lax.rem(t // 2, zs)
    x = t // (2 * zs)
    u = x * 2 + k
    up = lax.rem(c + 1, PEERS)
    down = lax.rem(c + PEERS - 1, PEERS)

    def z_peer(o):
        return (x * zs + lax.rem(z + o, zs)) * 2 + k

    def u_peer(o):
        v = lax.rem(u + o, us)
        return ((v // 2) * zs + z) * 2 + lax.rem(v, 2)

    lane = lax.broadcasted_iota(jnp.int32, (chp, LANES), 1)

    barrier = pltpu.get_barrier_semaphore()
    for o in range(1, PEERS):
        pl.semaphore_signal(barrier, inc=1, device_id=(t, lax.rem(c + o, PEERS)), device_id_type=MESH)
    for o in range(1, zs):
        pl.semaphore_signal(barrier, inc=1, device_id=(z_peer(o), c), device_id_type=MESH)
    for o in range(1, us):
        pl.semaphore_signal(barrier, inc=1, device_id=(u_peer(o), c), device_id_type=MESH)

    def remote(src, dst, send, recv, tile, chan):
        return pltpu.make_async_remote_copy(
            src_ref=src, dst_ref=dst, send_sem=send, recv_sem=recv, device_id=(tile, chan), device_id_type=MESH
        )

    def y_copy(layer, n, q):
        src, dst, chan = ((0, 3, up), (0, 1, down), (3, 2, up), (1, 2, down))[n]
        at = (pl.ds(q * part, part),) + (() if n < 2 else (n - 2,))
        return remote(
            share.at[(layer, src) + at],
            share.at[(layer, dst) + at],
            y_send.at[layer, n, q],
            y_recv.at[layer, n, q],
            t,
            chan,
        )

    def z_copy(layer, o):
        return remote(ring.at[layer], ring_z[layer].at[z], z_send.at[layer, o], z_recv.at[layer, o], z_peer(o), c)

    def u_copy(layer, o):
        return remote(
            slots.at[layer, lax.rem(u + o, us)],
            slots_x[layer].at[u],
            u_send.at[layer, o],
            u_recv.at[layer, o],
            u_peer(o),
            c,
        )

    def t_copy(o):
        return remote(table_own, table.at[u], t_send.at[o], t_recv.at[o], u_peer(o), c)

    def h_copy(layer, o):
        return remote(
            halo.at[layer, 0],
            halo.at[layer, PEERS - o],
            h_send.at[layer, o],
            h_recv.at[layer, o],
            t,
            lax.rem(c + o, PEERS),
        )

    flat[0 : ch * nr] = state[0].astype(f32).reshape(ch * nr, LANES)
    flat[ch * nr : chp * nr] = jnp.zeros(((chp - ch) * nr, LANES), f32)
    grid[...] = jnp.zeros(grid.shape, bf16)
    sides_k[...] = jnp.zeros(sides_k.shape, f32)

    def put_row(layer, i, h, row, sides):
        r = 2 * i + h
        row16 = row.astype(bf16)
        share[layer, 0, i, h] = row16
        grid[r + 1, 0:chp, :] = row16
        sides = jnp.where(lane == 1 + r, pltpu.roll(row, r + 2, 1), sides)
        return jnp.where(lane == 65 + r, pltpu.roll(row, r + 65, 1), sides)

    def mask_row(r):
        return wet[0, pl.ds(r, 1), :].astype(f32)

    def load_chunk(q, sides):
        for i in range(part):
            for h in range(2):
                r = 2 * (q * part + i) + h
                row = flat[pl.ds(r, chp, stride=nr), :] * mask_row(r)
                sides = put_row(0, q * part + i, h, row, sides)
        return sides

    def put_ring(layer, sides):
        ring[layer, :, 0:LANES] = share[layer, 0, 0, 0]
        ring[layer, :, LANES : 2 * LANES] = share[layer, 0, pairs - 1, 1]
        ring[layer, :, 2 * LANES : 3 * LANES] = sides.astype(bf16)

    def send_own(layer, q):
        for n in range(2):
            y_copy(layer, n, q).start()

    def send_ring(layer):
        for o in range(1, zs):
            z_copy(layer, o).start()

    put_ring(0, lax.fori_loop(0, CHUNKS, load_chunk, jnp.zeros((chp, LANES), f32)))
    table_own[...] = jnp.zeros((8, LANES), jnp.int32)
    table_own[0:1, 0:8] = nb[...] * 2 + fold[...]

    pl.semaphore_wait(barrier, (PEERS - 1) + (zs - 1) + (us - 1))
    send_ring(0)
    for q in range(2):
        send_own(0, q)
    for o in range(1, us):
        t_copy(o).start()

    k_in = lax.broadcasted_iota(jnp.int32, (PEERS * ch, depth), 0)
    k_at = lax.broadcasted_iota(jnp.int32, (PEERS * ch, depth), 1)
    place = jnp.zeros((PEERS * ch, depth), jnp.bool_)
    for j in range(PEERS):
        owner = lax.rem(c + j, PEERS)
        place = place | ((k_at - SLOT * j == k_in - ch * owner) & (k_at >= SLOT * j) & (k_at < SLOT * j + ch))
    place = jnp.where(place, 1.0, 0.0).astype(bf16)
    taps_f[...] = jnp.zeros(taps_f.shape, f32)
    for layer, w in enumerate((w1, w2)):
        for a in range(3):
            for b in range(3):
                taps_f[b * chp : b * chp + ch, a * depth : (a + 1) * depth] = jnp.dot(
                    w[3 * a + b], place, preferred_element_type=f32
                )
        taps[layer] = taps_f[...].astype(bf16)

    eye = lax.broadcasted_iota(jnp.int32, (chp, ch), 0) == lax.broadcasted_iota(jnp.int32, (chp, ch), 1)

    def bias_column(b):
        spread = jnp.broadcast_to(b[...], (chp, ch))
        return jnp.sum(jnp.where(eye, spread, 0.0), axis=1, keepdims=True)

    biases = bias_column(b1), bias_column(b2)
    flip = jnp.where(
        lax.broadcasted_iota(jnp.int32, (LANES, LANES), 0) + lax.broadcasted_iota(jnp.int32, (LANES, LANES), 1)
        == LANES - 1,
        1.0,
        0.0,
    ).astype(bf16)

    table[u] = table_own[...]
    for o in range(1, us):
        t_copy(o).wait_recv()
    move = pltpu.make_async_copy(table, table_s, local_sem)
    move.start()
    move.wait()

    east, west = (lane >= 65) & (lane < 65 + nr), (lane >= 1) & (lane < 1 + nr)
    sides_at = slice(2 * LANES, 3 * LANES)

    def read_table(v):
        codes = [table_s[v, 0, n] for n in range(8)]
        return [code >> 1 for code in codes], [code & 1 for code in codes]

    def build_slot(layer, v):
        ids, folds = read_table(v)
        at = [lax.rem(jnp.maximum(q, 0) // 2, zs) for q in ids]
        slots[layer, v, :, 0:LANES] = ring_z[layer][at[1], :, LANES : 2 * LANES]
        plain = ring_z[layer][at[0], :, 0:LANES]
        folded = ring_z[layer][at[0], :, LANES : 2 * LANES]
        slots[layer, v, :, LANES : 2 * LANES] = jnp.where(folds[0] == 1, folded, plain)

        def sides(n):
            return ring_z[layer][at[n], :, sides_at].astype(f32)

        def corner_top(n):
            v = sides(n)
            return jnp.where(folds[n] == 1, pltpu.roll(v, 65, 1), pltpu.roll(v, nr, 1))

        result = jnp.where(east, sides(2), sides(3))
        result = jnp.where(lane == 65 + nr, corner_top(4), result)
        result = jnp.where(lane == 1 + nr, corner_top(5), result)
        result = jnp.where(lane == 64, pltpu.roll(sides(6), LANES - nr, 1), result)
        result = jnp.where(lane == 0, pltpu.roll(sides(7), LANES - nr, 1), result)
        slots[layer, v, :, sides_at] = result.astype(bf16)

    def merge(layer):
        ids, folds = read_table(u)
        at = [(jnp.maximum(q, 0) // (2 * zs)) * 2 + lax.rem(jnp.maximum(q, 0), 2) for q in ids]

        def usable(n, value):
            return jnp.where(ids[n] >= 0, value, jnp.zeros_like(value))

        halo[layer, 0, :, 0:LANES] = usable(1, slots_x[layer][at[1], :, 0:LANES])
        north = slots_x[layer][at[0], :, LANES : 2 * LANES]
        turned = jnp.dot(north, flip, preferred_element_type=f32).astype(bf16)
        halo[layer, 0, :, LANES : 2 * LANES] = usable(0, jnp.where(folds[0] == 1, turned, north))

        def sides(n):
            return usable(n, slots_x[layer][at[n], :, sides_at].astype(f32))

        result = jnp.where(east, sides(2), 0.0)
        result = jnp.where(west, sides(3), result)
        result = jnp.where(lane == 65 + nr, sides(4), result)
        result = jnp.where(lane == 1 + nr, sides(5), result)
        result = jnp.where(lane == 64, sides(6), result)
        result = jnp.where(lane == 0, sides(7), result)
        halo[layer, 0, :, sides_at] = result.astype(bf16)

    def gather(layer, q):
        for n in range(2):
            y_copy(layer, n, q).wait_recv()
            y_copy(layer, n + 2, q).start()
        if q + 2 < CHUNKS:
            send_own(layer, q + 2)

    def conv_rows(layer, columns):
        stacked = jnp.concatenate(
            [jnp.concatenate([column[a] for column in columns], axis=1) for a in range(3)], axis=0
        )
        return jnp.dot(taps[layer], stacked, preferred_element_type=f32)

    def add_columns(total):
        left = jnp.where(lane == 0, 0.0, pltpu.roll(total[0:chp], 1, 1))
        right = jnp.where(lane == LANES - 1, 0.0, pltpu.roll(total[2 * chp : 3 * chp], LANES - 1, 1))
        return total[chp : 2 * chp] + left + right

    def conv_chunk(layer, q, low, count):
        for n in range(2, 4):
            y_copy(layer, n, q).wait_recv()

        def pack(i, carry):
            for h in range(2):
                for j in range(1, PEERS):
                    grid[1 + 2 * i + h, j * SLOT : j * SLOT + chp, :] = share[layer, j, i, h]
            return carry

        lax.fori_loop(q * part, (q + 1) * part, pack, 0)
        total = conv_rows(layer, [[grid[low + n + a] for a in range(3)] for n in range(count)])
        for n in range(count):
            sums[low + n] = add_columns(total[:, n * LANES : (n + 1) * LANES])

    def layer_sums(layer):
        gather(layer, 0)
        gather(layer, 1)
        ring_z[layer][z] = ring[layer]
        for o in range(1, zs):
            z_copy(layer, o).wait_recv()

        def one_slot(v, carry):
            build_slot(layer, v)
            return carry

        lax.fori_loop(0, us, one_slot, 0)
        for o in range(1, us):
            u_copy(layer, o).start()
        slots_x[layer][u] = slots[layer, u]
        gather(layer, 2)
        conv_chunk(layer, 0, 1, rows_of - 2)
        gather(layer, 3)
        for o in range(1, us):
            u_copy(layer, o).wait_recv()
        merge(layer)
        for o in range(1, PEERS):
            h_copy(layer, o).start()
        for q in range(1, CHUNKS):
            conv_chunk(layer, q, q * rows_of - 1, rows_of)
        for o in range(1, PEERS):
            h_copy(layer, o).wait_recv()
        for j in range(PEERS):
            block = slice(j * SLOT, j * SLOT + chp)
            grid[0, block, :] = halo[layer, j, :, 0:LANES]
            grid[nr + 1, block, :] = halo[layer, j, :, LANES : 2 * LANES]
            sides_k[block, :] = halo[layer, j, :, sides_at].astype(f32)
        column = [pltpu.roll(sides_k[...], shift, 1).astype(bf16) if shift else sides_k[...].astype(bf16) for shift in (1, 0, LANES - 1)]
        total = conv_rows(layer, [[grid[r + a] for a in range(3)] for r in (0, nr - 1)] + [column])
        sums[0] = add_columns(total[:, 0:LANES])
        sums[nr - 1] = add_columns(total[:, LANES : 2 * LANES])
        return total[0:chp, sides_at], total[2 * chp : 3 * chp, sides_at]

    def full_row(r, to_west, to_east):
        edge = jnp.where(lane == 0, pltpu.roll(to_west, LANES - 1 - r, 1), 0.0)
        edge = jnp.where(lane == LANES - 1, pltpu.roll(to_east, 62 - r, 1), edge)
        return sums[r] + edge

    to_west, to_east = layer_sums(0)

    def hidden_chunk(q, sides):
        for i in range(part):
            for h in range(2):
                r = 2 * (q * part + i) + h
                v = full_row(r, to_west, to_east) + biases[0]
                v = 0.5 * v * (1.0 + jnp.tanh(math.sqrt(2.0 / math.pi) * (v + 0.044715 * (v * v * v))))
                sides = put_row(1, q * part + i, h, v * mask_row(r), sides)
        return sides

    def hidden_and_send(q, sides):
        sides = hidden_chunk(q, sides)
        send_own(1, q)
        return sides

    sides = lax.fori_loop(0, 2, hidden_and_send, jnp.zeros((chp, LANES), f32))
    put_ring(1, lax.fori_loop(2, CHUNKS, hidden_chunk, sides))
    send_ring(1)

    to_west, to_east = layer_sums(1)

    def final_chunk(q, carry):
        for i in range(part):
            for h in range(2):
                r = 2 * (q * part + i) + h
                own = share[0, 0, q * part + i, h].astype(f32)
                v = own + full_row(r, to_west, to_east) + biases[1]
                flat[pl.ds(r, chp, stride=nr), :] = v * mask_row(r)
        return carry

    lax.fori_loop(0, CHUNKS, final_chunk, 0)
    out[0] = flat[0 : ch * nr].reshape(ch, nr, LANES).astype(bf16)

    for o in range(1, us):
        t_copy(o).wait_send()
    for layer in range(2):
        for n in range(4):
            for q in range(CHUNKS):
                y_copy(layer, n, q).wait_send()
        for o in range(1, zs):
            z_copy(layer, o).wait_send()
        for o in range(1, us):
            u_copy(layer, o).wait_send()
        for o in range(1, PEERS):
            h_copy(layer, o).wait_send()


def build(mesh, xs, zs):
    us = 2 * xs

    def body(state, w1, b1, w2, b2, wet, nb, fold):
        ch, nr = state.shape[1], state.shape[2]
        chp = -(-ch // 8) * 8
        pairs = nr // 2
        f32, bf16 = jnp.float32, jnp.bfloat16
        vmem, dma = pltpu.VMEM, pltpu.SemaphoreType.DMA
        inside = pl.BlockSpec(memory_space=pltpu.VMEM)
        return pl.pallas_call(
            functools.partial(body_kernel, (xs, zs, ch, chp, nr)),
            out_shape=jax.ShapeDtypeStruct(state.shape, bf16),
            in_specs=[inside] * 8,
            out_specs=inside,
            scratch_shapes=[
                vmem((chp * nr, LANES), f32),
                vmem((2, PEERS, pairs, 2, chp, LANES), bf16),
                vmem((nr + 2, PEERS * SLOT, LANES), bf16),
                vmem((PEERS * SLOT, LANES), f32),
                vmem((3 * chp, 3 * PEERS * SLOT), f32),
                vmem((2, 3 * chp, 3 * PEERS * SLOT), bf16),
                vmem((nr, chp, LANES), f32),
                vmem((2, chp, 3 * LANES), bf16),
                vmem((zs, chp, 3 * LANES), bf16),
                vmem((zs, chp, 3 * LANES), bf16),
                vmem((2, us, chp, 3 * LANES), bf16),
                vmem((us, chp, 3 * LANES), bf16),
                vmem((us, chp, 3 * LANES), bf16),
                vmem((2, PEERS, chp, 3 * LANES), bf16),
                vmem((8, LANES), jnp.int32),
                vmem((us, 8, LANES), jnp.int32),
                pltpu.SMEM((us, 8, LANES), jnp.int32),
                dma((2, 4, CHUNKS)),
                dma((2, 4, CHUNKS)),
                dma((2, PEERS)),
                dma((2, PEERS)),
                dma((2, zs)),
                dma((2, zs)),
                dma((2, us)),
                dma((2, us)),
                dma((us,)),
                dma((us,)),
                dma,
            ],
            compiler_params=pltpu.CompilerParams(
                collective_id=0, has_side_effects=True, vmem_limit_bytes=48 * 1024 * 1024
            ),
        )(
            state,
            jnp.swapaxes(w1, 1, 2),
            b1.reshape(1, -1),
            jnp.swapaxes(w2, 1, 2),
            b2.reshape(1, -1),
            wet,
            nb,
            fold,
        )

    return jax.shard_map(
        body,
        mesh=mesh,
        in_specs=(
            P("tiles", "chan", None, None),
            P(None, None, "chan"),
            P("chan"),
            P(None, None, "chan"),
            P("chan"),
            P("tiles", None, None),
            P("tiles", None),
            P("tiles", None),
        ),
        out_specs=P("tiles", "chan", None, None),
        check_vma=False,
    )


def solution(mesh):
    return build(mesh, X_SIZE, Z_SIZE)
```

time: 66.8 us -> 61.9 us (0.927)
  Pallas kernels: 63.6 us -> 56.5 us
  local copies, waits for them, and re-layouts: 3.03 us -> 5.06 us
    pallas_call x1, Pallas kernels: 63.6 us -> 56.5 us  [body(): pl.pallas_call(functools.partial(body_kernel, (xs, zs, ch, chp, nr)), out...]
    unnamed x17, local copies, waits for them, and re-layouts: 3.03 us -> 5.06 us
where the time goes in v2:
time: 61.9 us; the launch traced here: 61.6 us
  Pallas kernels  56.5 us (91%)
  local copies, waits for them, and re-layouts  5.06 us (8%)
    pallas_call x1, Pallas kernels, body(): pl.pallas_call(functools.partial(body_kernel, (xs, zs, ch, chp, nr)), out...  56.5 us
    unnamed x17, local copies, waits for them, and re-layouts  5.06 us

profile of v2, /device:TPU:1, one launch (start us, length us, event | category | flops | bytes accessed | tf_op | source)
XLA Modules:
  0.0 61.6 jit_solution(5324883282193360913)
XLA Ops:
  0.0 0.0 copy-start.7
  0.0 0.0 copy-start.4
  0.0 0.0 copy-start.5
  0.0 0.0 copy-start.6
  0.0 0.6 %copy-done.7 = s32[1,8]{1,0:T(1,128)S(1)} copy-done((s32[1,8]{1,0:T(1,128)S(1)}, s32[1,8]{1,0:T(1,128)}, u32[]{:S(2)}) %copy-start.7) | copy-done | bytes 56
  0.7 0.0 copy-done.4
  0.7 0.0 copy-done.5
  0.7 0.0 copy-done.6
  0.7 0.0 copy-start
  0.7 1.0 %copy-done = bf16[1,50,32,128]{3,2,1,0:T(8,128)(2,1)S(1)} copy-done((bf16[1,50,32,128]{3,2,1,0:T(8,128)(2,1)S(1)}, bf16[1,50,32,128]{3,2,1,0:T(8,128)(2,1)}, u32[]{:S(2)}) %copy-start) | copy-done | bytes 409624
  1.7 0.0 copy-start.1
  1.7 0.9 %copy-done.1 = bf16[9,200,50]{1,2,0:T(8,128)(2,1)S(1)} copy-done((bf16[9,200,50]{1,2,0:T(8,128)(2,1)S(1)}, bf16[9,200,50]{1,2,0:T(8,128)(2,1)}, u32[]{:S(2)}) %copy-start.1) | copy-done | bytes 180024
  2.7 0.0 copy-start.2
  2.7 0.9 %copy-done.2 = bf16[9,200,50]{1,2,0:T(8,128)(2,1)S(1)} copy-done((bf16[9,200,50]{1,2,0:T(8,128)(2,1)S(1)}, bf16[9,200,50]{1,2,0:T(8,128)(2,1)}, u32[]{:S(2)}) %copy-start.2) | copy-done | bytes 180024
  3.6 0.0 copy-start.3
  3.6 0.7 %copy-done.3 = s32[1,32,128]{2,1,0:T(8,128)S(1)} copy-done((s32[1,32,128]{2,1,0:T(8,128)S(1)}, s32[1,32,128]{2,1,0:T(8,128)}, u32[]{:S(2)}) %copy-start.3) | copy-done | bytes 16408
  4.3 56.5 %shard_map.82 = bf16[1,50,32,128]{3,2,1,0:T(8,128)(2,1)S(1)} custom-call(bf16[1,50,32,128]{3,2,1,0:T(8,128)(2,1)S(1)} %copy-done, bf16[9,50,200]{2,1,0:T(8,128)(2,1)S(1)} %bitcast.4, f32[1,50]{1,0:T(1,128)S(1)} %bitcast.6, bf16[9,50,200]{2,1,0:T(8,128)(2,1)S(1)} %bitcast.5, f32[1,50]{1,0:T(1,128)S(1)} %bitcast.7, s32[1,32,128]{2,1,0:T(8,128)S(1)} %copy-done.3, ...), custom_call_target="tpu_custom_call" | custom-call | tf_op jit(solution)/shard_map/pallas_call | solution.py:409
  60.9 0.8 %copy.10 = bf16[1,50,32,128]{3,2,1,0:T(8,128)(2,1)} copy(bf16[1,50,32,128]{3,2,1,0:T(8,128)(2,1)S(1)} %shard_map.82) | data formatting | bytes 819200
Async XLA Ops:
  0.0 0.7 %copy-start.7 = (s32[1,8]{1,0:T(1,128)S(1)}, s32[1,8]{1,0:T(1,128)}, u32[]{:S(2)}) copy-start(s32[1,8]{1,0:T(1,128)} %fold.1) | copy-start | bytes 100
  0.0 0.7 %copy-start.4 = (f32[50]{0:T(128)S(1)}, f32[50]{0:T(128)}, u32[]{:S(2)}) copy-start(f32[50]{0:T(128)} %param.10) | copy-start | bytes 604
  0.0 0.7 %copy-start.5 = (f32[50]{0:T(128)S(1)}, f32[50]{0:T(128)}, u32[]{:S(2)}) copy-start(f32[50]{0:T(128)} %param.12) | copy-start | bytes 604
  0.0 0.7 %copy-start.6 = (s32[1,8]{1,0:T(1,128)S(1)}, s32[1,8]{1,0:T(1,128)}, u32[]{:S(2)}) copy-start(s32[1,8]{1,0:T(1,128)} %nb.1) | copy-start | bytes 100
  0.7 1.0 %copy-start = (bf16[1,50,32,128]{3,2,1,0:T(8,128)(2,1)S(1)}, bf16[1,50,32,128]{3,2,1,0:T(8,128)(2,1)}, u32[]{:S(2)}) copy-start(bf16[1,50,32,128]{3,2,1,0:T(8,128)(2,1)} %state.1) | copy-start | bytes 1228804
  1.7 0.9 %copy-start.1 = (bf16[9,200,50]{1,2,0:T(8,128)(2,1)S(1)}, bf16[9,200,50]{1,2,0:T(8,128)(2,1)}, u32[]{:S(2)}) copy-start(bf16[9,200,50]{1,2,0:T(8,128)(2,1)} %param.9) | copy-start | bytes 540004
  2.7 0.9 %copy-start.2 = (bf16[9,200,50]{1,2,0:T(8,128)(2,1)S(1)}, bf16[9,200,50]{1,2,0:T(8,128)(2,1)}, u32[]{:S(2)}) copy-start(bf16[9,200,50]{1,2,0:T(8,128)(2,1)} %param.11) | copy-start | bytes 540004
  3.6 0.7 %copy-start.3 = (s32[1,32,128]{2,1,0:T(8,128)S(1)}, s32[1,32,128]{2,1,0:T(8,128)}, u32[]{:S(2)}) copy-start(s32[1,32,128]{2,1,0:T(8,128)} %wet.1) | copy-start | bytes 49156

commit v3 on v2

v3 whole, which is shorter than its diff:
```python
import functools
import math

import jax
import jax.numpy as jnp
from jax import lax
from jax.experimental import pallas as pl
from jax.experimental.pallas import tpu as pltpu
from jax.sharding import PartitionSpec as P

MESH = pl.DeviceIdType.MESH
LANES = 128
SLOT = 64
PEERS = 4
X_SIZE = 4
Z_SIZE = 8
CHUNKS = 4


def body_kernel(
    geo,
    state_at,
    w1_at,
    b1_at,
    w2_at,
    b2_at,
    wet_at,
    nb_at,
    fold_at,
    out,
    state,
    w1,
    b1,
    w2,
    b2,
    wet,
    nb,
    fold,
    flat,
    share,
    grid,
    sides_k,
    taps_f,
    taps,
    sums,
    ring_z0,
    ring_z1,
    slots,
    slots_x0,
    slots_x1,
    halo,
    table_own,
    table,
    table_s,
    y_send,
    y_recv,
    h_send,
    h_recv,
    z_send,
    z_recv,
    s_send,
    s_recv,
    u_send,
    u_recv,
    t_send,
    t_recv,
    local_sem,
):
    xs, zs, ch, chp, nr = geo
    ring_z, slots_x = (ring_z0, ring_z1), (slots_x0, slots_x1)
    pairs = nr // 2
    part = pairs // CHUNKS
    rows_of = 2 * part
    depth = PEERS * SLOT
    f32, bf16 = jnp.float32, jnp.bfloat16

    t = lax.axis_index("tiles")
    c = lax.axis_index("chan")
    k = lax.rem(t, 2)
    z = lax.rem(t // 2, zs)
    x = t // (2 * zs)
    me = z * 2 + k
    up = lax.rem(c + 1, PEERS)
    down = lax.rem(c + PEERS - 1, PEERS)

    def along_z(o):
        return lax.rem(z + o + zs, zs) * 2 + k

    def z_peer(o):
        return x * zs * 2 + along_z(o)

    def x_peer(o):
        return lax.rem(x + o, xs) * zs * 2 + me

    sibling = t + 1 - 2 * k
    copies = [
        pltpu.make_async_copy(src, dst, local_sem.at[n])
        for n, (src, dst) in enumerate(
            (
                (state_at, state),
                (wet_at, wet),
                (nb_at, nb),
                (fold_at, fold),
                (w1_at, w1),
                (w2_at, w2),
                (b1_at, b1),
                (b2_at, b2),
            )
        )
    ]
    for copy in copies:
        copy.start()
    lane = lax.broadcasted_iota(jnp.int32, (chp, LANES), 1)

    barrier = pltpu.get_barrier_semaphore()
    for o in range(1, PEERS):
        pl.semaphore_signal(barrier, inc=1, device_id=(t, lax.rem(c + o, PEERS)), device_id_type=MESH)
    tiles = [z_peer(o) for o in (2, -2, 1, -1)] + [x_peer(o) for o in range(1, xs)] + [sibling]
    for tile in tiles:
        pl.semaphore_signal(barrier, inc=1, device_id=(tile, c), device_id_type=MESH)

    def remote(src, dst, send, recv, tile, chan):
        return pltpu.make_async_remote_copy(
            src_ref=src, dst_ref=dst, send_sem=send, recv_sem=recv, device_id=(tile, chan), device_id_type=MESH
        )

    def y_copy(layer, n, q):
        src, dst, chan = ((0, 3, up), (0, 1, down), (3, 2, up), (1, 2, down))[n]
        at = (pl.ds(q * part, part),) + (() if n < 2 else (n - 2,))
        return remote(
            share.at[(layer, src) + at],
            share.at[(layer, dst) + at],
            y_send.at[layer, n, q],
            y_recv.at[layer, n, q],
            t,
            chan,
        )

    def z_copy(layer, n):
        origin, target, tiles_of = (
            (0, 2, None),
            (0, -2, None),
            (0, 1, None),
            (0, -1, None),
            (-2, 1, None),
            (2, -1, None),
            (-2, 2, pl.ds(0, 2)),
            (2, -2, pl.ds(2, 1)),
        )[n]
        at = (along_z(origin),) + (() if tiles_of is None else (tiles_of,))
        return remote(
            ring_z[layer].at[at], ring_z[layer].at[at], z_send.at[layer, n], z_recv.at[layer, n], z_peer(target), c
        )

    def s_copy(layer, o, mine=True):
        at = along_z(o) if mine else along_z(o) + 1 - 2 * k
        return remote(ring_z[layer].at[at], ring_z[layer].at[at], s_send.at[layer, o], s_recv.at[layer, o], sibling, c)

    def u_copy(layer, o):
        return remote(
            slots.at[layer, lax.rem(x + o, xs)],
            slots_x[layer].at[x],
            u_send.at[layer, o],
            u_recv.at[layer, o],
            x_peer(o),
            c,
        )

    def t_copy(o):
        return remote(table_own, table.at[x], t_send.at[o], t_recv.at[o], x_peer(o), c)

    def h_copy(layer, o):
        return remote(
            halo.at[layer, 0],
            halo.at[layer, PEERS - o],
            h_send.at[layer, o],
            h_recv.at[layer, o],
            t,
            lax.rem(c + o, PEERS),
        )

    grid[...] = jnp.zeros(grid.shape, bf16)
    sides_k[...] = jnp.zeros(sides_k.shape, f32)
    table_own[...] = jnp.zeros((8, LANES), jnp.int32)
    for n in range(4):
        copies[n].wait()
    table_own[0:1, 0:8] = nb[...] * 2 + fold[...]
    flat[0 : ch * nr] = state[0].astype(f32).reshape(ch * nr, LANES)
    flat[ch * nr : chp * nr] = jnp.zeros(((chp - ch) * nr, LANES), f32)

    def put_row(layer, i, h, row, sides):
        r = 2 * i + h
        row16 = row[0:ch].astype(bf16)
        share[layer, 0, i, h] = row16
        grid[r + 1, 0:ch, :] = row16
        sides = jnp.where(lane == 1 + r, pltpu.roll(row, r + 2, 1), sides)
        return jnp.where(lane == 65 + r, pltpu.roll(row, r + 65, 1), sides)

    def mask_row(r):
        return wet[0, pl.ds(r, 1), :].astype(f32)

    def load_chunk(q, sides):
        for i in range(part):
            for h in range(2):
                r = 2 * (q * part + i) + h
                row = flat[pl.ds(r, chp, stride=nr), :] * mask_row(r)
                sides = put_row(0, q * part + i, h, row, sides)
        return sides

    def put_ring(layer, sides):
        ring_z[layer][me, 0] = share[layer, 0, 0, 0]
        ring_z[layer][me, 1] = share[layer, 0, pairs - 1, 1]
        ring_z[layer][me, 2] = sides[0:ch].astype(bf16)

    def send_own(layer, q):
        for n in range(2):
            y_copy(layer, n, q).start()

    def send_ring(layer):
        for n in range(4):
            z_copy(layer, n).start()
        s_copy(layer, 0).start()

    put_ring(0, lax.fori_loop(0, CHUNKS, load_chunk, jnp.zeros((chp, LANES), f32)))
    pl.semaphore_wait(barrier, PEERS - 1 + len(tiles))
    send_ring(0)
    for q in range(2):
        send_own(0, q)
    for o in range(1, xs):
        t_copy(o).start()

    k_in = lax.broadcasted_iota(jnp.int32, (PEERS * ch, depth), 0)
    k_at = lax.broadcasted_iota(jnp.int32, (PEERS * ch, depth), 1)
    place = jnp.zeros((PEERS * ch, depth), jnp.bool_)
    for j in range(PEERS):
        owner = lax.rem(c + j, PEERS)
        place = place | ((k_at - SLOT * j == k_in - ch * owner) & (k_at >= SLOT * j) & (k_at < SLOT * j + ch))
    place = jnp.where(place, 1.0, 0.0).astype(bf16)
    taps_f[...] = jnp.zeros(taps_f.shape, f32)
    for n in range(4, 8):
        copies[n].wait()
    for layer, w in enumerate((w1, w2)):
        for a in range(3):
            for b in range(3):
                taps_f[b * chp : b * chp + ch, a * depth : (a + 1) * depth] = jnp.dot(
                    w[3 * a + b], place, preferred_element_type=f32
                )
        taps[layer] = taps_f[...].astype(bf16)

    eye = lax.broadcasted_iota(jnp.int32, (chp, ch), 0) == lax.broadcasted_iota(jnp.int32, (chp, ch), 1)

    def bias_column(b):
        spread = jnp.broadcast_to(b[...], (chp, ch))
        return jnp.sum(jnp.where(eye, spread, 0.0), axis=1, keepdims=True)

    biases = bias_column(b1), bias_column(b2)
    flip = jnp.where(
        lax.broadcasted_iota(jnp.int32, (LANES, LANES), 0) + lax.broadcasted_iota(jnp.int32, (LANES, LANES), 1)
        == LANES - 1,
        1.0,
        0.0,
    ).astype(bf16)

    table[x] = table_own[...]
    for o in range(1, xs):
        t_copy(o).wait_recv()
    move = pltpu.make_async_copy(table, table_s, local_sem.at[8])
    move.start()
    move.wait()

    lane_ch = lax.broadcasted_iota(jnp.int32, (ch, LANES), 1)
    east = (lane_ch >= 65) & (lane_ch < 65 + nr)
    west = (lane_ch >= 1) & (lane_ch < 1 + nr)

    def read_table(v):
        codes = [table_s[v, 0, n] for n in range(8)]
        return [code >> 1 for code in codes], [code & 1 for code in codes]

    def build_slot(layer, v):
        ids, folds = read_table(v)
        at = [lax.rem(jnp.maximum(q, 0), 2 * zs) for q in ids]
        slots[layer, v, 0] = ring_z[layer][at[1], 1]
        slots[layer, v, 1] = jnp.where(folds[0] == 1, ring_z[layer][at[0], 1], ring_z[layer][at[0], 0])

        def sides(n):
            return ring_z[layer][at[n], 2].astype(f32)

        def corner_top(n):
            v = sides(n)
            return jnp.where(folds[n] == 1, pltpu.roll(v, 65, 1), pltpu.roll(v, nr, 1))

        result = jnp.where(east, sides(2), sides(3))
        result = jnp.where(lane_ch == 65 + nr, corner_top(4), result)
        result = jnp.where(lane_ch == 1 + nr, corner_top(5), result)
        result = jnp.where(lane_ch == 64, pltpu.roll(sides(6), LANES - nr, 1), result)
        result = jnp.where(lane_ch == 0, pltpu.roll(sides(7), LANES - nr, 1), result)
        slots[layer, v, 2] = result.astype(bf16)

    def merge(layer):
        ids, folds = read_table(x)
        at = [jnp.maximum(q, 0) // (2 * zs) for q in ids]

        def usable(n, value):
            return jnp.where(ids[n] >= 0, value, jnp.zeros_like(value))

        halo[layer, 0, 0] = usable(1, slots_x[layer][at[1], 0])
        north = slots_x[layer][at[0], 1]
        turned = jnp.dot(north, flip, preferred_element_type=f32).astype(bf16)
        halo[layer, 0, 1] = usable(0, jnp.where(folds[0] == 1, turned, north))

        def sides(n):
            return usable(n, slots_x[layer][at[n], 2].astype(f32))

        result = jnp.where(east, sides(2), 0.0)
        result = jnp.where(west, sides(3), result)
        result = jnp.where(lane_ch == 65 + nr, sides(4), result)
        result = jnp.where(lane_ch == 1 + nr, sides(5), result)
        result = jnp.where(lane_ch == 64, sides(6), result)
        result = jnp.where(lane_ch == 0, sides(7), result)
        halo[layer, 0, 2] = result.astype(bf16)

    def gather(layer, q):
        for n in range(2):
            y_copy(layer, n, q).wait_recv()
            y_copy(layer, n + 2, q).start()
        if q + 2 < CHUNKS:
            send_own(layer, q + 2)

    def conv_rows(layer, columns):
        stacked = jnp.concatenate(
            [jnp.concatenate([column[a] for column in columns], axis=1) for a in range(3)], axis=0
        )
        return jnp.dot(taps[layer], stacked, preferred_element_type=f32)

    def add_columns(total):
        left = jnp.where(lane == 0, 0.0, pltpu.roll(total[0:chp], 1, 1))
        right = jnp.where(lane == LANES - 1, 0.0, pltpu.roll(total[2 * chp : 3 * chp], LANES - 1, 1))
        return total[chp : 2 * chp] + left + right

    def conv_chunk(layer, q, low, count):
        for n in range(2, 4):
            y_copy(layer, n, q).wait_recv()

        def pack(i, carry):
            for h in range(2):
                for j in range(1, PEERS):
                    grid[1 + 2 * i + h, j * SLOT : j * SLOT + ch, :] = share[layer, j, i, h]
            return carry

        lax.fori_loop(q * part, (q + 1) * part, pack, 0)
        total = conv_rows(layer, [[grid[low + n + a] for a in range(3)] for n in range(count)])
        for n in range(count):
            sums[low + n] = add_columns(total[:, n * LANES : (n + 1) * LANES])

    def layer_sums(layer):
        z_copy(layer, 0).wait_recv()
        z_copy(layer, 4).start()
        z_copy(layer, 6).start()
        z_copy(layer, 1).wait_recv()
        z_copy(layer, 5).start()
        z_copy(layer, 7).start()
        s_copy(layer, zs - 2).start()
        s_copy(layer, 2).start()
        for n, o in ((2, zs - 1), (3, 1)):
            z_copy(layer, n).wait_recv()
            s_copy(layer, o).start()
        gather(layer, 0)
        for n, o in ((4, zs - 3), (5, 3)):
            z_copy(layer, n).wait_recv()
            s_copy(layer, o).start()
        z_copy(layer, 6).wait_recv()
        z_copy(layer, 7).wait_recv()
        s_copy(layer, 4).start()
        gather(layer, 1)
        for o in range(zs):
            s_copy(layer, o, False).wait_recv()

        def one_slot(v, carry):
            build_slot(layer, v)
            return carry

        lax.fori_loop(0, xs, one_slot, 0)
        for o in range(1, xs):
            u_copy(layer, o).start()
        slots_x[layer][x] = slots[layer, x]
        gather(layer, 2)
        conv_chunk(layer, 0, 1, rows_of - 2)
        for o in range(1, xs):
            u_copy(layer, o).wait_recv()
        merge(layer)
        for o in range(1, PEERS):
            h_copy(layer, o).start()
        gather(layer, 3)
        for q in range(1, CHUNKS):
            conv_chunk(layer, q, q * rows_of - 1, rows_of)
        for o in range(1, PEERS):
            h_copy(layer, o).wait_recv()
        for j in range(PEERS):
            block = slice(j * SLOT, j * SLOT + ch)
            grid[0, block, :] = halo[layer, j, 0]
            grid[nr + 1, block, :] = halo[layer, j, 1]
            sides_k[block, :] = halo[layer, j, 2].astype(f32)
        column = [pltpu.roll(sides_k[...], shift, 1).astype(bf16) if shift else sides_k[...].astype(bf16) for shift in (1, 0, LANES - 1)]
        total = conv_rows(layer, [[grid[r + a] for a in range(3)] for r in (0, nr - 1)] + [column])
        sums[0] = add_columns(total[:, 0:LANES])
        sums[nr - 1] = add_columns(total[:, LANES : 2 * LANES])
        return total[0:chp, 2 * LANES :], total[2 * chp : 3 * chp, 2 * LANES :]

    def full_row(r, to_west, to_east):
        edge = jnp.where(lane == 0, pltpu.roll(to_west, LANES - 1 - r, 1), 0.0)
        edge = jnp.where(lane == LANES - 1, pltpu.roll(to_east, 62 - r, 1), edge)
        return sums[r] + edge

    to_west, to_east = layer_sums(0)

    def hidden_chunk(q, sides):
        for i in range(part):
            for h in range(2):
                r = 2 * (q * part + i) + h
                v = full_row(r, to_west, to_east) + biases[0]
                v = 0.5 * v * (1.0 + jnp.tanh(math.sqrt(2.0 / math.pi) * (v + 0.044715 * (v * v * v))))
                sides = put_row(1, q * part + i, h, v * mask_row(r), sides)
        return sides

    def hidden_and_send(q, sides):
        sides = hidden_chunk(q, sides)
        send_own(1, q)
        return sides

    sides = lax.fori_loop(0, 2, hidden_and_send, jnp.zeros((chp, LANES), f32))
    put_ring(1, lax.fori_loop(2, CHUNKS, hidden_chunk, sides))
    send_ring(1)

    to_west, to_east = layer_sums(1)

    def final_chunk(q, carry):
        for i in range(part):
            for h in range(2):
                r = 2 * (q * part + i) + h
                own = share[0, 0, q * part + i, h].astype(f32)
                v = own + (full_row(r, to_west, to_east) + biases[1])[0:ch]
                flat[pl.ds(r, ch, stride=nr), :] = v * mask_row(r)
        return carry

    lax.fori_loop(0, CHUNKS, final_chunk, 0)
    out[0] = flat[0 : ch * nr].reshape(ch, nr, LANES).astype(bf16)

    for o in range(1, xs):
        t_copy(o).wait_send()
    for layer in range(2):
        for n in range(4):
            for q in range(CHUNKS):
                y_copy(layer, n, q).wait_send()
        for n in range(8):
            z_copy(layer, n).wait_send()
        for o in range(zs):
            s_copy(layer, o).wait_send()
        for o in range(1, xs):
            u_copy(layer, o).wait_send()
        for o in range(1, PEERS):
            h_copy(layer, o).wait_send()


def build(mesh, xs, zs):
    def body(state, w1, b1, w2, b2, wet, nb, fold):
        ch, nr = state.shape[1], state.shape[2]
        chp = -(-ch // 8) * 8
        pairs = nr // 2
        f32, bf16 = jnp.float32, jnp.bfloat16
        vmem, dma = pltpu.VMEM, pltpu.SemaphoreType.DMA
        inside = pl.BlockSpec(memory_space=pltpu.VMEM)
        return pl.pallas_call(
            functools.partial(body_kernel, (xs, zs, ch, chp, nr)),
            out_shape=jax.ShapeDtypeStruct(state.shape, bf16),
            in_specs=[pl.BlockSpec(memory_space=pl.ANY)] * 8,
            out_specs=inside,
            scratch_shapes=[
                vmem(state.shape, bf16),
                vmem((9, ch, PEERS * ch), bf16),
                vmem((1, ch), f32),
                vmem((9, ch, PEERS * ch), bf16),
                vmem((1, ch), f32),
                vmem(wet.shape, jnp.int32),
                vmem(nb.shape, jnp.int32),
                vmem(fold.shape, jnp.int32),
                vmem((chp * nr, LANES), f32),
                vmem((2, PEERS, pairs, 2, ch, LANES), bf16),
                vmem((nr + 2, PEERS * SLOT, LANES), bf16),
                vmem((PEERS * SLOT, LANES), f32),
                vmem((3 * chp, 3 * PEERS * SLOT), f32),
                vmem((2, 3 * chp, 3 * PEERS * SLOT), bf16),
                vmem((nr, chp, LANES), f32),
                vmem((2 * zs, 3, ch, LANES), bf16),
                vmem((2 * zs, 3, ch, LANES), bf16),
                vmem((2, xs, 3, ch, LANES), bf16),
                vmem((xs, 3, ch, LANES), bf16),
                vmem((xs, 3, ch, LANES), bf16),
                vmem((2, PEERS, 3, ch, LANES), bf16),
                vmem((8, LANES), jnp.int32),
                vmem((xs, 8, LANES), jnp.int32),
                pltpu.SMEM((xs, 8, LANES), jnp.int32),
                dma((2, 4, CHUNKS)),
                dma((2, 4, CHUNKS)),
                dma((2, PEERS)),
                dma((2, PEERS)),
                dma((2, 8)),
                dma((2, 8)),
                dma((2, zs)),
                dma((2, zs)),
                dma((2, xs)),
                dma((2, xs)),
                dma((xs,)),
                dma((xs,)),
                dma((9,)),
            ],
            compiler_params=pltpu.CompilerParams(
                collective_id=0, has_side_effects=True, vmem_limit_bytes=63 * 1024 * 1024
            ),
        )(
            state,
            jnp.swapaxes(w1, 1, 2),
            b1.reshape(1, -1),
            jnp.swapaxes(w2, 1, 2),
            b2.reshape(1, -1),
            wet,
            nb,
            fold,
        )

    return jax.shard_map(
        body,
        mesh=mesh,
        in_specs=(
            P("tiles", "chan", None, None),
            P(None, None, "chan"),
            P("chan"),
            P(None, None, "chan"),
            P("chan"),
            P("tiles", None, None),
            P("tiles", None),
            P("tiles", None),
        ),
        out_specs=P("tiles", "chan", None, None),
        check_vma=False,
    )


def solution(mesh):
    return build(mesh, X_SIZE, Z_SIZE)
```

time: 61.9 us -> 57.7 us (0.932)
  local copies, waits for them, and re-layouts: 5.06 us -> 1.78 us
  Pallas kernels: 56.5 us -> 55.8 us
    unnamed x17 -> x1, local copies, waits for them, and re-layouts: 5.06 us -> 1.78 us
    pallas_call x1, Pallas kernels: 56.5 us -> 55.8 us  [body(): pl.pallas_call(functools.partial(body_kernel, (xs, zs, ch, chp, nr)), out...]
where the time goes in v3:
time: 57.7 us; the launch traced here: 57.6 us
  Pallas kernels  55.8 us (97%)
  local copies, waits for them, and re-layouts  1.78 us (3%)
    pallas_call x1, Pallas kernels, body(): pl.pallas_call(functools.partial(body_kernel, (xs, zs, ch, chp, nr)), out...  55.8 us
    unnamed x1, local copies, waits for them, and re-layouts  1.78 us

profile of v3, /device:TPU:1, one launch (start us, length us, event | category | flops | bytes accessed | tf_op | source)
XLA Modules:
  0.0 57.6 jit_solution(6009159478993693406)
XLA Ops:
  0.0 55.8 %shard_map.82 = bf16[1,50,32,128]{3,2,1,0:T(8,128)(2,1)} custom-call(bf16[1,50,32,128]{3,2,1,0:T(8,128)(2,1)} %state_at.1, bf16[9,50,200]{2,1,0:T(8,128)(2,1)} %bitcast.4, f32[1,50]{1,0:T(1,128)} %bitcast.6, bf16[9,50,200]{2,1,0:T(8,128)(2,1)} %bitcast.5, f32[1,50]{1,0:T(1,128)} %bitcast.7, s32[1,32,128]{2,1,0:T(8,128)} %wet_at.1, s32[1,8]{1,0:T(1,128)} %nb_at.1, ...), custom_call_target="tpu_custom_call" | custom-call | tf_op jit(solution)/shard_map/pallas_call | solution.py:472
  55.8 1.8 %copy.10 = bf16[1,50,32,128]{3,2,1,0:T(8,128)(2,1)} copy(bf16[1,50,32,128]{3,2,1,0:T(8,128)(2,1)} %shard_map.82) | data formatting | bytes 819200

commit v4 on v3

--- a/solution.py
+++ b/solution.py
@@ -43,11 +43,16 @@
     taps_f,
     taps,
     sums,
-    ring_z0,
-    ring_z1,
-    slots,
-    slots_x0,
-    slots_x1,
+    rows_0,
+    rows_1,
+    cols_0,
+    cols_1,
+    slots_rows,
+    slots_cols,
+    rows_x0,
+    rows_x1,
+    cols_x0,
+    cols_x1,
     halo,
     table_own,
     table,
@@ -67,7 +72,10 @@
     local_sem,
 ):
     xs, zs, ch, chp, nr = geo
-    ring_z, slots_x = (ring_z0, ring_z1), (slots_x0, slots_x1)
+    ring = (rows_0, cols_0), (rows_1, cols_1)
+    slots = slots_rows, slots_cols
+    slots_x = (rows_x0, cols_x0), (rows_x1, cols_x1)
+    halo_at = pl.ds(0, 2), pl.ds(2, 1)
     pairs = nr // 2
     part = pairs // CHUNKS
     rows_of = 2 * part
@@ -136,32 +144,25 @@
             chan,
         )
 
-    def z_copy(layer, n):
-        origin, target, tiles_of = (
-            (0, 2, None),
-            (0, -2, None),
-            (0, 1, None),
-            (0, -1, None),
-            (-2, 1, None),
-            (2, -1, None),
-            (-2, 2, pl.ds(0, 2)),
-            (2, -2, pl.ds(2, 1)),
-        )[n]
-        at = (along_z(origin),) + (() if tiles_of is None else (tiles_of,))
+    def z_copy(layer, n, p):
+        origin, target = ((0, 2), (0, -2), (0, 1), (0, -1), (-2, 1), (2, -1), (-2, 2), (2, -2))[n]
+        at = (along_z(origin),) + ((pl.ds(n - 6, 1),) if n >= 6 and p == 0 else ())
+        where = ring[layer][p].at[at]
+        return remote(where, where, z_send.at[layer, p, n], z_recv.at[layer, p, n], z_peer(target), c)
+
+    def far_copies(layer, p):
+        return [z_copy(layer, n, p) for n in ((6, 7) if p == 0 else (7,))]
+
+    def s_copy(layer, o, p, mine=True):
+        where = ring[layer][p].at[along_z(o) if mine else along_z(o) + 1 - 2 * k]
+        return remote(where, where, s_send.at[layer, p, o], s_recv.at[layer, p, o], sibling, c)
+
+    def u_copy(layer, o, p):
         return remote(
-            ring_z[layer].at[at], ring_z[layer].at[at], z_send.at[layer, n], z_recv.at[layer, n], z_peer(target), c
-        )
-
-    def s_copy(layer, o, mine=True):
-        at = along_z(o) if mine else along_z(o) + 1 - 2 * k
-        return remote(ring_z[layer].at[at], ring_z[layer].at[at], s_send.at[layer, o], s_recv.at[layer, o], sibling, c)
-
-    def u_copy(layer, o):
-        return remote(
-            slots.at[layer, lax.rem(x + o, xs)],
-            slots_x[layer].at[x],
-            u_send.at[layer, o],
-            u_recv.at[layer, o],
+            slots[p].at[layer, lax.rem(x + o, xs)],
+            slots_x[layer][p].at[x],
+            u_send.at[layer, p, o],
+            u_recv.at[layer, p, o],
             x_peer(o),
             c,
         )
@@ -169,12 +170,12 @@
     def t_copy(o):
         return remote(table_own, table.at[x], t_send.at[o], t_recv.at[o], x_peer(o), c)
 
-    def h_copy(layer, o):
+    def h_copy(layer, o, p):
         return remote(
-            halo.at[layer, 0],
-            halo.at[layer, PEERS - o],
-            h_send.at[layer, o],
-            h_recv.at[layer, o],
+            halo.at[layer, 0, halo_at[p]],
+            halo.at[layer, PEERS - o, halo_at[p]],
+            h_send.at[layer, p, o],
+            h_recv.at[layer, p, o],
             t,
             lax.rem(c + o, PEERS),
         )
@@ -207,23 +208,23 @@
                 sides = put_row(0, q * part + i, h, row, sides)
         return sides
 
-    def put_ring(layer, sides):
-        ring_z[layer][me, 0] = share[layer, 0, 0, 0]
-        ring_z[layer][me, 1] = share[layer, 0, pairs - 1, 1]
-        ring_z[layer][me, 2] = sides[0:ch].astype(bf16)
-
     def send_own(layer, q):
         for n in range(2):
             y_copy(layer, n, q).start()
 
-    def send_ring(layer):
+    def send_ring(layer, p):
         for n in range(4):
-            z_copy(layer, n).start()
-        s_copy(layer, 0).start()
-
-    put_ring(0, lax.fori_loop(0, CHUNKS, load_chunk, jnp.zeros((chp, LANES), f32)))
+            z_copy(layer, n, p).start()
+        s_copy(layer, 0, p).start()
+
+    sides = lax.fori_loop(0, CHUNKS, load_chunk, jnp.zeros((chp, LANES), f32))
+    rows_0[me, 0] = share[0, 0, 0, 0]
+    rows_0[me, 1] = share[0, 0, pairs - 1, 1]
+    cols_0[me, 0] = sides[0:ch].astype(bf16)
+
     pl.semaphore_wait(barrier, PEERS - 1 + len(tiles))
-    send_ring(0)
+    for p in range(2):
+        send_ring(0, p)
     for q in range(2):
         send_own(0, q)
     for o in range(1, xs):
@@ -276,55 +277,64 @@
         codes = [table_s[v, 0, n] for n in range(8)]
         return [code >> 1 for code in codes], [code & 1 for code in codes]
 
-    def build_slot(layer, v):
+    def build_rows(layer, v):
+        ids, folds = read_table(v)
+        north, south = [lax.rem(jnp.maximum(q, 0), 2 * zs) for q in ids[0:2]]
+        edges = ring[layer][0]
+        slots_rows[layer, v, 0] = edges[south, 1]
+        slots_rows[layer, v, 1] = jnp.where(folds[0] == 1, edges[north, 1], edges[north, 0])
+
+    def build_cols(layer, v):
         ids, folds = read_table(v)
         at = [lax.rem(jnp.maximum(q, 0), 2 * zs) for q in ids]
-        slots[layer, v, 0] = ring_z[layer][at[1], 1]
-        slots[layer, v, 1] = jnp.where(folds[0] == 1, ring_z[layer][at[0], 1], ring_z[layer][at[0], 0])
-
-        def sides(n):
-            return ring_z[layer][at[n], 2].astype(f32)
+
+        def cols(n):
+            return ring[layer][1][at[n], 0].astype(f32)
 
         def corner_top(n):
-            v = sides(n)
+            v = cols(n)
             return jnp.where(folds[n] == 1, pltpu.roll(v, 65, 1), pltpu.roll(v, nr, 1))
 
-        result = jnp.where(east, sides(2), sides(3))
+        result = jnp.where(east, cols(2), cols(3))
         result = jnp.where(lane_ch == 65 + nr, corner_top(4), result)
         result = jnp.where(lane_ch == 1 + nr, corner_top(5), result)
-        result = jnp.where(lane_ch == 64, pltpu.roll(sides(6), LANES - nr, 1), result)
-        result = jnp.where(lane_ch == 0, pltpu.roll(sides(7), LANES - nr, 1), result)
-        slots[layer, v, 2] = result.astype(bf16)
-
-    def merge(layer):
+        result = jnp.where(lane_ch == 64, pltpu.roll(cols(6), LANES - nr, 1), result)
+        result = jnp.where(lane_ch == 0, pltpu.roll(cols(7), LANES - nr, 1), result)
+        slots_cols[layer, v, 0] = result.astype(bf16)
+
+    def usable(code, value):
+        return jnp.where(code >= 0, value, jnp.zeros_like(value))
+
+    def merge_rows(layer):
         ids, folds = read_table(x)
-        at = [jnp.maximum(q, 0) // (2 * zs) for q in ids]
-
-        def usable(n, value):
-            return jnp.where(ids[n] >= 0, value, jnp.zeros_like(value))
-
-        halo[layer, 0, 0] = usable(1, slots_x[layer][at[1], 0])
-        north = slots_x[layer][at[0], 1]
+        at = [jnp.maximum(q, 0) // (2 * zs) for q in ids[0:2]]
+        edges = slots_x[layer][0]
+        halo[layer, 0, 0] = usable(ids[1], edges[at[1], 0])
+        north = edges[at[0], 1]
         turned = jnp.dot(north, flip, preferred_element_type=f32).astype(bf16)
-        halo[layer, 0, 1] = usable(0, jnp.where(folds[0] == 1, turned, north))
-
-        def sides(n):
-            return usable(n, slots_x[layer][at[n], 2].astype(f32))
-
-        result = jnp.where(east, sides(2), 0.0)
-        result = jnp.where(west, sides(3), result)
-        result = jnp.where(lane_ch == 65 + nr, sides(4), result)
-        result = jnp.where(lane_ch == 1 + nr, sides(5), result)
-        result = jnp.where(lane_ch == 64, sides(6), result)
-        result = jnp.where(lane_ch == 0, sides(7), result)
+        halo[layer, 0, 1] = usable(ids[0], jnp.where(folds[0] == 1, turned, north))
+
+    def merge_cols(layer):
+        ids, _ = read_table(x)
+
+        def cols(n):
+            return usable(ids[n], slots_x[layer][1][jnp.maximum(ids[n], 0) // (2 * zs), 0].astype(f32))
+
+        result = jnp.where(east, cols(2), 0.0)
+        result = jnp.where(west, cols(3), result)
+        result = jnp.where(lane_ch == 65 + nr, cols(4), result)
+        result = jnp.where(lane_ch == 1 + nr, cols(5), result)
+        result = jnp.where(lane_ch == 64, cols(6), result)
+        result = jnp.where(lane_ch == 0, cols(7), result)
         halo[layer, 0, 2] = result.astype(bf16)
 
     def gather(layer, q):
         for n in range(2):
             y_copy(layer, n, q).wait_recv()
             y_copy(layer, n + 2, q).start()
-        if q + 2 < CHUNKS:
-            send_own(layer, q + 2)
+        if q == 0:
+            for later in range(2, CHUNKS):
+                send_own(layer, later)
 
     def conv_rows(layer, columns):
         stacked = jnp.concatenate(
@@ -353,48 +363,66 @@
             sums[low + n] = add_columns(total[:, n * LANES : (n + 1) * LANES])
 
     def layer_sums(layer):
-        z_copy(layer, 0).wait_recv()
-        z_copy(layer, 4).start()
-        z_copy(layer, 6).start()
-        z_copy(layer, 1).wait_recv()
-        z_copy(layer, 5).start()
-        z_copy(layer, 7).start()
-        s_copy(layer, zs - 2).start()
-        s_copy(layer, 2).start()
-        for n, o in ((2, zs - 1), (3, 1)):
-            z_copy(layer, n).wait_recv()
-            s_copy(layer, o).start()
+        def near(p):
+            z_copy(layer, 0, p).wait_recv()
+            z_copy(layer, 4, p).start()
+            if p == 0:
+                z_copy(layer, 6, p).start()
+            z_copy(layer, 1, p).wait_recv()
+            z_copy(layer, 5, p).start()
+            z_copy(layer, 7, p).start()
+            s_copy(layer, zs - 2, p).start()
+            s_copy(layer, 2, p).start()
+            for n, o in ((2, zs - 1), (3, 1)):
+                z_copy(layer, n, p).wait_recv()
+                s_copy(layer, o, p).start()
+
+        def far(p):
+            for n, o in ((4, zs - 3), (5, 3)):
+                z_copy(layer, n, p).wait_recv()
+                s_copy(layer, o, p).start()
+            for copy in far_copies(layer, p):
+                copy.wait_recv()
+            s_copy(layer, 4, p).start()
+
+        def along_x(p):
+            for o in range(zs):
+                s_copy(layer, o, p, False).wait_recv()
+
+            def one_slot(v, carry):
+                (build_rows, build_cols)[p](layer, v)
+                return carry
+
+            lax.fori_loop(0, xs, one_slot, 0)
+            for o in range(1, xs):
+                u_copy(layer, o, p).start()
+            slots_x[layer][p][x] = slots[p][layer, x]
+
+        def along_y(p):
+            for o in range(1, xs):
+                u_copy(layer, o, p).wait_recv()
+            (merge_rows, merge_cols)[p](layer)
+            for o in range(1, PEERS):
+                h_copy(layer, o, p).start()
+
+        near(0)
+        near(1)
         gather(layer, 0)
-        for n, o in ((4, zs - 3), (5, 3)):
-            z_copy(layer, n).wait_recv()
-            s_copy(layer, o).start()
-        z_copy(layer, 6).wait_recv()
-        z_copy(layer, 7).wait_recv()
-        s_copy(layer, 4).start()
+        far(0)
+        far(1)
         gather(layer, 1)
-        for o in range(zs):
-            s_copy(layer, o, False).wait_recv()
-
-        def one_slot(v, carry):
-            build_slot(layer, v)
-            return carry
-
-        lax.fori_loop(0, xs, one_slot, 0)
-        for o in range(1, xs):
-            u_copy(layer, o).start()
-        slots_x[layer][x] = slots[layer, x]
+        along_x(0)
+        along_x(1)
         gather(layer, 2)
+        along_y(0)
+        along_y(1)
         conv_chunk(layer, 0, 1, rows_of - 2)
-        for o in range(1, xs):
-            u_copy(layer, o).wait_recv()
-        merge(layer)
-        for o in range(1, PEERS):
-            h_copy(layer, o).start()
         gather(layer, 3)
         for q in range(1, CHUNKS):
             conv_chunk(layer, q, q * rows_of - 1, rows_of)
-        for o in range(1, PEERS):
-            h_copy(layer, o).wait_recv()
+        for p in range(2):
+            for o in range(1, PEERS):
+                h_copy(layer, o, p).wait_recv()
         for j in range(PEERS):
             block = slice(j * SLOT, j * SLOT + ch)
             grid[0, block, :] = halo[layer, j, 0]
@@ -413,13 +441,15 @@
 
     to_west, to_east = layer_sums(0)
 
+    def hidden_row(r):
+        v = full_row(r, to_west, to_east) + biases[0]
+        v = 0.5 * v * (1.0 + jnp.tanh(math.sqrt(2.0 / math.pi) * (v + 0.044715 * (v * v * v))))
+        return v * mask_row(r)
+
     def hidden_chunk(q, sides):
         for i in range(part):
             for h in range(2):
-                r = 2 * (q * part + i) + h
-                v = full_row(r, to_west, to_east) + biases[0]
-                v = 0.5 * v * (1.0 + jnp.tanh(math.sqrt(2.0 / math.pi) * (v + 0.044715 * (v * v * v))))
-                sides = put_row(1, q * part + i, h, v * mask_row(r), sides)
+                sides = put_row(1, q * part + i, h, hidden_row(2 * (q * part + i) + h), sides)
         return sides
 
     def hidden_and_send(q, sides):
@@ -427,9 +457,13 @@
         send_own(1, q)
         return sides
 
+    rows_1[me, 0] = hidden_row(0)[0:ch].astype(bf16)
+    rows_1[me, 1] = hidden_row(nr - 1)[0:ch].astype(bf16)
+    send_ring(1, 0)
     sides = lax.fori_loop(0, 2, hidden_and_send, jnp.zeros((chp, LANES), f32))
-    put_ring(1, lax.fori_loop(2, CHUNKS, hidden_chunk, sides))
-    send_ring(1)
+    sides = lax.fori_loop(2, CHUNKS, hidden_chunk, sides)
+    cols_1[me, 0] = sides[0:ch].astype(bf16)
+    send_ring(1, 1)
 
     to_west, to_east = layer_sums(1)
 
@@ -451,14 +485,17 @@
         for n in range(4):
             for q in range(CHUNKS):
                 y_copy(layer, n, q).wait_send()
-        for n in range(8):
-            z_copy(layer, n).wait_send()
-        for o in range(zs):
-            s_copy(layer, o).wait_send()
-        for o in range(1, xs):
-            u_copy(layer, o).wait_send()
-        for o in range(1, PEERS):
-            h_copy(layer, o).wait_send()
+        for p in range(2):
+            for n in range(6):
+                z_copy(layer, n, p).wait_send()
+            for copy in far_copies(layer, p):
+                copy.wait_send()
+            for o in range(zs):
+                s_copy(layer, o, p).wait_send()
+            for o in range(1, xs):
+                u_copy(layer, o, p).wait_send()
+            for o in range(1, PEERS):
+                h_copy(layer, o, p).wait_send()
 
 
 def build(mesh, xs, zs):
@@ -490,25 +527,30 @@
                 vmem((3 * chp, 3 * PEERS * SLOT), f32),
                 vmem((2, 3 * chp, 3 * PEERS * SLOT), bf16),
                 vmem((nr, chp, LANES), f32),
-                vmem((2 * zs, 3, ch, LANES), bf16),
-                vmem((2 * zs, 3, ch, LANES), bf16),
-                vmem((2, xs, 3, ch, LANES), bf16),
-                vmem((xs, 3, ch, LANES), bf16),
-                vmem((xs, 3, ch, LANES), bf16),
+                vmem((2 * zs, 2, ch, LANES), bf16),
+                vmem((2 * zs, 2, ch, LANES), bf16),
+                vmem((2 * zs, 1, ch, LANES), bf16),
+                vmem((2 * zs, 1, ch, LANES), bf16),
+                vmem((2, xs, 2, ch, LANES), bf16),
+                vmem((2, xs, 1, ch, LANES), bf16),
+                vmem((xs, 2, ch, LANES), bf16),
+                vmem((xs, 2, ch, LANES), bf16),
+                vmem((xs, 1, ch, LANES), bf16),
+                vmem((xs, 1, ch, LANES), bf16),
                 vmem((2, PEERS, 3, ch, LANES), bf16),
                 vmem((8, LANES), jnp.int32),
                 vmem((xs, 8, LANES), jnp.int32),
                 pltpu.SMEM((xs, 8, LANES), jnp.int32),
                 dma((2, 4, CHUNKS)),
                 dma((2, 4, CHUNKS)),
-                dma((2, PEERS)),
-                dma((2, PEERS)),
-                dma((2, 8)),
-                dma((2, 8)),
-                dma((2, zs)),
-                dma((2, zs)),
-                dma((2, xs)),
-                dma((2, xs)),
+                dma((2, 2, PEERS)),
+                dma((2, 2, PEERS)),
+                dma((2, 2, 8)),
+                dma((2, 2, 8)),
+                dma((2, 2, zs)),
+                dma((2, 2, zs)),
+                dma((2, 2, xs)),
+                dma((2, 2, xs)),
                 dma((xs,)),
                 dma((xs,)),
                 dma((9,)),

time: 57.7 us -> 55.7 us (0.965)
  Pallas kernels: 55.8 us -> 53.8 us
    pallas_call x1, Pallas kernels: 55.8 us -> 53.8 us  [body(): pl.pallas_call(functools.partial(body_kernel, (xs, zs, ch, chp, nr)), out...]
where the time goes in v4:
time: 55.7 us; the launch traced here: 55.6 us
  Pallas kernels  53.8 us (97%)
  local copies, waits for them, and re-layouts  1.78 us (3%)
    pallas_call x1, Pallas kernels, body(): pl.pallas_call(functools.partial(body_kernel, (xs, zs, ch, chp, nr)), out...  53.8 us
    unnamed x1, local copies, waits for them, and re-layouts  1.78 us

profile of v4, /device:TPU:1, one launch (start us, length us, event | category | flops | bytes accessed | tf_op | source)
XLA Modules:
  0.0 55.6 jit_solution(2073551412306039716)
XLA Ops:
  0.0 53.8 %shard_map.82 = bf16[1,50,32,128]{3,2,1,0:T(8,128)(2,1)} custom-call(bf16[1,50,32,128]{3,2,1,0:T(8,128)(2,1)} %state_at.1, bf16[9,50,200]{2,1,0:T(8,128)(2,1)} %bitcast.4, f32[1,50]{1,0:T(1,128)} %bitcast.6, bf16[9,50,200]{2,1,0:T(8,128)(2,1)} %bitcast.5, f32[1,50]{1,0:T(1,128)} %bitcast.7, s32[1,32,128]{2,1,0:T(8,128)} %wet_at.1, s32[1,8]{1,0:T(1,128)} %nb_at.1, ...), custom_call_target="tpu_custom_call" | custom-call | tf_op jit(solution)/shard_map/pallas_call | solution.py:509
  53.8 1.8 %copy.10 = bf16[1,50,32,128]{3,2,1,0:T(8,128)(2,1)} copy(bf16[1,50,32,128]{3,2,1,0:T(8,128)(2,1)} %shard_map.82) | data formatting | bytes 819200

commit v5 on v4

--- a/solution.py
+++ b/solution.py
@@ -194,8 +194,7 @@
         row16 = row[0:ch].astype(bf16)
         share[layer, 0, i, h] = row16
         grid[r + 1, 0:ch, :] = row16
-        sides = jnp.where(lane == 1 + r, pltpu.roll(row, r + 2, 1), sides)
-        return jnp.where(lane == 65 + r, pltpu.roll(row, r + 65, 1), sides)
+        return jnp.where((lane == 2 * r + 3) | (lane == 2 * r + 4), pltpu.roll(row, 2 * r + 4, 1), sides)
 
     def mask_row(r):
         return wet[0, pl.ds(r, 1), :].astype(f32)
@@ -225,7 +224,7 @@
     pl.semaphore_wait(barrier, PEERS - 1 + len(tiles))
     for p in range(2):
         send_ring(0, p)
-    for q in range(2):
+    for q in range(CHUNKS):
         send_own(0, q)
     for o in range(1, xs):
         t_copy(o).start()
@@ -270,8 +269,9 @@
     move.wait()
 
     lane_ch = lax.broadcasted_iota(jnp.int32, (ch, LANES), 1)
-    east = (lane_ch >= 65) & (lane_ch < 65 + nr)
-    west = (lane_ch >= 1) & (lane_ch < 1 + nr)
+    odd = (lane_ch & 1) == 1
+    east = (~odd) & (lane_ch >= 4) & (lane_ch <= 2 * nr + 2)
+    west = odd & (lane_ch >= 3) & (lane_ch <= 2 * nr + 1)
 
     def read_table(v):
         codes = [table_s[v, 0, n] for n in range(8)]
@@ -291,15 +291,15 @@
         def cols(n):
             return ring[layer][1][at[n], 0].astype(f32)
 
-        def corner_top(n):
+        def corner_top(n, across):
             v = cols(n)
-            return jnp.where(folds[n] == 1, pltpu.roll(v, 65, 1), pltpu.roll(v, nr, 1))
-
-        result = jnp.where(east, cols(2), cols(3))
-        result = jnp.where(lane_ch == 65 + nr, corner_top(4), result)
-        result = jnp.where(lane_ch == 1 + nr, corner_top(5), result)
-        result = jnp.where(lane_ch == 64, pltpu.roll(cols(6), LANES - nr, 1), result)
-        result = jnp.where(lane_ch == 0, pltpu.roll(cols(7), LANES - nr, 1), result)
+            return jnp.where(folds[n] == 1, pltpu.roll(v, across, 1), pltpu.roll(v, 2 * nr, 1))
+
+        result = jnp.where(odd, cols(3), cols(2))
+        result = jnp.where(lane_ch == 2 * nr + 4, corner_top(4, 3), result)
+        result = jnp.where(lane_ch == 2 * nr + 3, corner_top(5, 1), result)
+        result = jnp.where(lane_ch == 2, pltpu.roll(cols(6), LANES - 2 * nr, 1), result)
+        result = jnp.where(lane_ch == 1, pltpu.roll(cols(7), LANES - 2 * nr, 1), result)
         slots_cols[layer, v, 0] = result.astype(bf16)
 
     def usable(code, value):
@@ -322,19 +322,16 @@
 
         result = jnp.where(east, cols(2), 0.0)
         result = jnp.where(west, cols(3), result)
-        result = jnp.where(lane_ch == 65 + nr, cols(4), result)
-        result = jnp.where(lane_ch == 1 + nr, cols(5), result)
-        result = jnp.where(lane_ch == 64, cols(6), result)
-        result = jnp.where(lane_ch == 0, cols(7), result)
+        result = jnp.where(lane_ch == 2 * nr + 4, cols(4), result)
+        result = jnp.where(lane_ch == 2 * nr + 3, cols(5), result)
+        result = jnp.where(lane_ch == 2, cols(6), result)
+        result = jnp.where(lane_ch == 1, cols(7), result)
         halo[layer, 0, 2] = result.astype(bf16)
 
     def gather(layer, q):
         for n in range(2):
             y_copy(layer, n, q).wait_recv()
             y_copy(layer, n + 2, q).start()
-        if q == 0:
-            for later in range(2, CHUNKS):
-                send_own(layer, later)
 
     def conv_rows(layer, columns):
         stacked = jnp.concatenate(
@@ -407,17 +404,17 @@
 
         near(0)
         near(1)
+        far(0)
         gather(layer, 0)
-        far(0)
         far(1)
+        along_x(0)
         gather(layer, 1)
-        along_x(0)
         along_x(1)
         gather(layer, 2)
         along_y(0)
+        gather(layer, 3)
         along_y(1)
         conv_chunk(layer, 0, 1, rows_of - 2)
-        gather(layer, 3)
         for q in range(1, CHUNKS):
             conv_chunk(layer, q, q * rows_of - 1, rows_of)
         for p in range(2):
@@ -428,28 +425,34 @@
             grid[0, block, :] = halo[layer, j, 0]
             grid[nr + 1, block, :] = halo[layer, j, 1]
             sides_k[block, :] = halo[layer, j, 2].astype(f32)
-        column = [pltpu.roll(sides_k[...], shift, 1).astype(bf16) if shift else sides_k[...].astype(bf16) for shift in (1, 0, LANES - 1)]
+        frame = sides_k[...]
+        column = [v.astype(bf16) for v in (pltpu.roll(frame, 2, 1), frame, pltpu.roll(frame, LANES - 2, 1))]
         total = conv_rows(layer, [[grid[r + a] for a in range(3)] for r in (0, nr - 1)] + [column])
         sums[0] = add_columns(total[:, 0:LANES])
         sums[nr - 1] = add_columns(total[:, LANES : 2 * LANES])
-        return total[0:chp, 2 * LANES :], total[2 * chp : 3 * chp, 2 * LANES :]
-
-    def full_row(r, to_west, to_east):
-        edge = jnp.where(lane == 0, pltpu.roll(to_west, LANES - 1 - r, 1), 0.0)
-        edge = jnp.where(lane == LANES - 1, pltpu.roll(to_east, 62 - r, 1), edge)
-        return sums[r] + edge
-
-    to_west, to_east = layer_sums(0)
-
-    def hidden_row(r):
-        v = full_row(r, to_west, to_east) + biases[0]
+        return jnp.where((lane & 1) == 1, total[0:chp, 2 * LANES :], total[2 * chp : 3 * chp, 2 * LANES :])
+
+    def turn(columns, r):
+        return pltpu.roll(columns, 123 - 2 * r, 1)
+
+    def full_row(r, below, this):
+        return sums[r] + jnp.where(lane == 0, below, jnp.where(lane == LANES - 1, this, 0.0))
+
+    columns_0 = layer_sums(0)
+
+    def hidden_row(r, below, this):
+        v = full_row(r, below, this) + biases[0]
         v = 0.5 * v * (1.0 + jnp.tanh(math.sqrt(2.0 / math.pi) * (v + 0.044715 * (v * v * v))))
         return v * mask_row(r)
 
     def hidden_chunk(q, sides):
+        below = turn(columns_0, q * rows_of - 1)
         for i in range(part):
             for h in range(2):
-                sides = put_row(1, q * part + i, h, hidden_row(2 * (q * part + i) + h), sides)
+                r = 2 * (q * part + i) + h
+                this = turn(columns_0, r)
+                sides = put_row(1, q * part + i, h, hidden_row(r, below, this), sides)
+                below = this
         return sides
 
     def hidden_and_send(q, sides):
@@ -457,23 +460,25 @@
         send_own(1, q)
         return sides
 
-    rows_1[me, 0] = hidden_row(0)[0:ch].astype(bf16)
-    rows_1[me, 1] = hidden_row(nr - 1)[0:ch].astype(bf16)
+    for n, r in enumerate((0, nr - 1)):
+        rows_1[me, n] = hidden_row(r, turn(columns_0, r - 1), turn(columns_0, r))[0:ch].astype(bf16)
     send_ring(1, 0)
-    sides = lax.fori_loop(0, 2, hidden_and_send, jnp.zeros((chp, LANES), f32))
-    sides = lax.fori_loop(2, CHUNKS, hidden_chunk, sides)
+    sides = lax.fori_loop(0, CHUNKS, hidden_and_send, jnp.zeros((chp, LANES), f32))
     cols_1[me, 0] = sides[0:ch].astype(bf16)
     send_ring(1, 1)
 
-    to_west, to_east = layer_sums(1)
+    columns_1 = layer_sums(1)
 
     def final_chunk(q, carry):
+        below = turn(columns_1, q * rows_of - 1)
         for i in range(part):
             for h in range(2):
                 r = 2 * (q * part + i) + h
+                this = turn(columns_1, r)
                 own = share[0, 0, q * part + i, h].astype(f32)
-                v = own + (full_row(r, to_west, to_east) + biases[1])[0:ch]
+                v = own + (full_row(r, below, this) + biases[1])[0:ch]
                 flat[pl.ds(r, ch, stride=nr), :] = v * mask_row(r)
+                below = this
         return carry
 
     lax.fori_loop(0, CHUNKS, final_chunk, 0)

time: 55.7 us -> 54.3 us (0.975)
  Pallas kernels: 53.8 us -> 52.4 us
    pallas_call x1, Pallas kernels: 53.8 us -> 52.4 us  [body(): pl.pallas_call(functools.partial(body_kernel, (xs, zs, ch, chp, nr)), out...]
where the time goes in v5:
time: 54.3 us; the launch traced here: 54.2 us
  Pallas kernels  52.4 us (97%)
  local copies, waits for them, and re-layouts  1.78 us (3%)
    pallas_call x1, Pallas kernels, body(): pl.pallas_call(functools.partial(body_kernel, (xs, zs, ch, chp, nr)), out...  52.4 us
    unnamed x1, local copies, waits for them, and re-layouts  1.78 us

profile of v5, /device:TPU:1, one launch (start us, length us, event | category | flops | bytes accessed | tf_op | source)
XLA Modules:
  0.0 54.2 jit_solution(5478293383874782910)
XLA Ops:
  0.0 52.4 %shard_map.82 = bf16[1,50,32,128]{3,2,1,0:T(8,128)(2,1)} custom-call(bf16[1,50,32,128]{3,2,1,0:T(8,128)(2,1)} %state_at.1, bf16[9,50,200]{2,1,0:T(8,128)(2,1)} %bitcast.4, f32[1,50]{1,0:T(1,128)} %bitcast.6, bf16[9,50,200]{2,1,0:T(8,128)(2,1)} %bitcast.5, f32[1,50]{1,0:T(1,128)} %bitcast.7, s32[1,32,128]{2,1,0:T(8,128)} %wet_at.1, s32[1,8]{1,0:T(1,128)} %nb_at.1, ...), custom_call_target="tpu_custom_call" | custom-call | tf_op jit(solution)/shard_map/pallas_call | solution.py:514
  52.4 1.8 %copy.10 = bf16[1,50,32,128]{3,2,1,0:T(8,128)(2,1)} copy(bf16[1,50,32,128]{3,2,1,0:T(8,128)(2,1)} %shard_map.82) | data formatting | bytes 819200

commit v6 on v5

--- a/solution.py
+++ b/solution.py
@@ -54,6 +54,10 @@
     cols_x0,
     cols_x1,
     halo,
+    fix,
+    fix_f,
+    mask_cols,
+    sums_cols,
     table_own,
     table,
     table_s,
@@ -61,6 +65,8 @@
     y_recv,
     h_send,
     h_recv,
+    f_send,
+    f_recv,
     z_send,
     z_recv,
     s_send,
@@ -180,6 +186,16 @@
             lax.rem(c + o, PEERS),
         )
 
+    def f_copy(o, p):
+        return remote(
+            fix.at[0, halo_at[p]],
+            fix.at[PEERS - o, halo_at[p]],
+            f_send.at[p, o],
+            f_recv.at[p, o],
+            t,
+            lax.rem(c + o, PEERS),
+        )
+
     grid[...] = jnp.zeros(grid.shape, bf16)
     sides_k[...] = jnp.zeros(sides_k.shape, f32)
     table_own[...] = jnp.zeros((8, LANES), jnp.int32)
@@ -189,23 +205,26 @@
     flat[0 : ch * nr] = state[0].astype(f32).reshape(ch * nr, LANES)
     flat[ch * nr : chp * nr] = jnp.zeros(((chp - ch) * nr, LANES), f32)
 
-    def put_row(layer, i, h, row, sides):
-        r = 2 * i + h
-        row16 = row[0:ch].astype(bf16)
-        share[layer, 0, i, h] = row16
-        grid[r + 1, 0:ch, :] = row16
-        return jnp.where((lane == 2 * r + 3) | (lane == 2 * r + 4), pltpu.roll(row, 2 * r + 4, 1), sides)
+    def put_cols(r, row, sides):
+        at = lax.broadcasted_iota(jnp.int32, row.shape, 1)
+        return jnp.where((at == 2 * r + 3) | (at == 2 * r + 4), pltpu.roll(row, 2 * r + 4, 1), sides)
 
     def mask_row(r):
         return wet[0, pl.ds(r, 1), :].astype(f32)
 
-    def load_chunk(q, sides):
+    def load_chunk(q, carry):
+        sides, wet_sides = carry
         for i in range(part):
             for h in range(2):
                 r = 2 * (q * part + i) + h
-                row = flat[pl.ds(r, chp, stride=nr), :] * mask_row(r)
-                sides = put_row(0, q * part + i, h, row, sides)
-        return sides
+                row_mask = mask_row(r)
+                row = flat[pl.ds(r, chp, stride=nr), :] * row_mask
+                row16 = row[0:ch].astype(bf16)
+                share[0, 0, q * part + i, h] = row16
+                grid[r + 1, 0:ch, :] = row16
+                sides = put_cols(r, row, sides)
+                wet_sides = put_cols(r, jnp.broadcast_to(row_mask, (8, LANES)), wet_sides)
+        return sides, wet_sides
 
     def send_own(layer, q):
         for n in range(2):
@@ -216,7 +235,13 @@
             z_copy(layer, n, p).start()
         s_copy(layer, 0, p).start()
 
-    sides = lax.fori_loop(0, CHUNKS, load_chunk, jnp.zeros((chp, LANES), f32))
+    sides, wet_sides = lax.fori_loop(
+        0, CHUNKS, load_chunk, (jnp.zeros((chp, LANES), f32), jnp.zeros((8, LANES), f32))
+    )
+    mask_cols[...] = wet_sides
+    sums_cols[...] = jnp.zeros((chp, LANES), f32)
+    sums[0] = jnp.zeros((chp, LANES), f32)
+    sums[nr - 1] = jnp.zeros((chp, LANES), f32)
     rows_0[me, 0] = share[0, 0, 0, 0]
     rows_0[me, 1] = share[0, 0, pairs - 1, 1]
     cols_0[me, 0] = sides[0:ch].astype(bf16)
@@ -350,14 +375,40 @@
 
         def pack(i, carry):
             for h in range(2):
-                for j in range(1, PEERS):
-                    grid[1 + 2 * i + h, j * SLOT : j * SLOT + ch, :] = share[layer, j, i, h]
+                for j in range(layer == 0, PEERS):
+                    row = share[layer, j, i, h]
+                    if layer == 1:
+                        ends = pltpu.roll(fix_f[j], LANES - 4 - 2 * (2 * i + h), 1)[0:ch].astype(bf16)
+                        row = jnp.where((lane_ch == 0) | (lane_ch == LANES - 1), ends, row)
+                    grid[1 + 2 * i + h, j * SLOT : j * SLOT + ch, :] = row
             return carry
 
         lax.fori_loop(q * part, (q + 1) * part, pack, 0)
+        if layer == 1 and q in (0, CHUNKS - 1):
+            for j in range(PEERS):
+                grid[nr if q else 1, j * SLOT : j * SLOT + ch, :] = fix[j, 1 if q else 0]
         total = conv_rows(layer, [[grid[low + n + a] for a in range(3)] for n in range(count)])
         for n in range(count):
             sums[low + n] = add_columns(total[:, n * LANES : (n + 1) * LANES])
+
+    def gelu(v):
+        v = v + biases[0]
+        return 0.5 * v * (1.0 + jnp.tanh(math.sqrt(2.0 / math.pi) * (v + 0.044715 * (v * v * v))))
+
+    def hidden_inside(q):
+        def one_part(i, carry):
+            cols = sums_cols[...]
+            for n in range(2):
+                for h in range(2):
+                    r = 2 * (2 * i + n) + h
+                    row = sums[r]
+                    share[1, 0, 2 * i + n, h] = (gelu(row) * mask_row(r))[0:ch].astype(bf16)
+                    cols = put_cols(r, row, cols)
+            sums_cols[...] = cols
+            return carry
+
+        lax.fori_loop(q * part // 2, (q + 1) * part // 2, one_part, 0)
+        send_own(1, q)
 
     def layer_sums(layer):
         def near(p):
@@ -414,9 +465,19 @@
         along_y(0)
         gather(layer, 3)
         along_y(1)
+        if layer == 1:
+            for p in range(2):
+                for o in range(1, PEERS):
+                    f_copy(o, p).wait_recv()
+            for j in range(PEERS):
+                fix_f[j, 0:ch, :] = fix[j, 2].astype(f32)
         conv_chunk(layer, 0, 1, rows_of - 2)
         for q in range(1, CHUNKS):
             conv_chunk(layer, q, q * rows_of - 1, rows_of)
+            if layer == 0:
+                hidden_inside(q - 1)
+        if layer == 0:
+            hidden_inside(CHUNKS - 1)
         for p in range(2):
             for o in range(1, PEERS):
                 h_copy(layer, o, p).wait_recv()
@@ -440,32 +501,22 @@
 
     columns_0 = layer_sums(0)
 
-    def hidden_row(r, below, this):
-        v = full_row(r, below, this) + biases[0]
-        v = 0.5 * v * (1.0 + jnp.tanh(math.sqrt(2.0 / math.pi) * (v + 0.044715 * (v * v * v))))
-        return v * mask_row(r)
-
-    def hidden_chunk(q, sides):
-        below = turn(columns_0, q * rows_of - 1)
-        for i in range(part):
-            for h in range(2):
-                r = 2 * (q * part + i) + h
-                this = turn(columns_0, r)
-                sides = put_row(1, q * part + i, h, hidden_row(r, below, this), sides)
-                below = this
-        return sides
-
-    def hidden_and_send(q, sides):
-        sides = hidden_chunk(q, sides)
-        send_own(1, q)
-        return sides
-
+    cols = sums_cols[...]
     for n, r in enumerate((0, nr - 1)):
-        rows_1[me, n] = hidden_row(r, turn(columns_0, r - 1), turn(columns_0, r))[0:ch].astype(bf16)
+        row = full_row(r, turn(columns_0, r - 1), turn(columns_0, r))
+        row16 = (gelu(row) * mask_row(r))[0:ch].astype(bf16)
+        rows_1[me, n] = row16
+        fix[0, n] = row16
+        cols = put_cols(r, sums[r], cols)
     send_ring(1, 0)
-    sides = lax.fori_loop(0, CHUNKS, hidden_and_send, jnp.zeros((chp, LANES), f32))
-    cols_1[me, 0] = sides[0:ch].astype(bf16)
+    frame = jnp.where((lane & 1) == 1, pltpu.roll(columns_0, LANES - 1, 1), pltpu.roll(columns_0, 1, 1))
+    cols16 = (gelu(cols + frame) * mask_cols[0:1, :])[0:ch].astype(bf16)
+    cols_1[me, 0] = cols16
+    fix[0, 2] = cols16
     send_ring(1, 1)
+    for p in range(2):
+        for o in range(1, PEERS):
+            f_copy(o, p).start()
 
     columns_1 = layer_sums(1)
 
@@ -486,6 +537,9 @@
 
     for o in range(1, xs):
         t_copy(o).wait_send()
+    for p in range(2):
+        for o in range(1, PEERS):
+            f_copy(o, p).wait_send()
     for layer in range(2):
         for n in range(4):
             for q in range(CHUNKS):
@@ -543,6 +597,10 @@
                 vmem((xs, 1, ch, LANES), bf16),
                 vmem((xs, 1, ch, LANES), bf16),
                 vmem((2, PEERS, 3, ch, LANES), bf16),
+                vmem((PEERS, 3, ch, LANES), bf16),
+                vmem((PEERS, chp, LANES), f32),
+                vmem((8, LANES), f32),
+                vmem((chp, LANES), f32),
                 vmem((8, LANES), jnp.int32),
                 vmem((xs, 8, LANES), jnp.int32),
                 pltpu.SMEM((xs, 8, LANES), jnp.int32),
@@ -550,6 +608,8 @@
                 dma((2, 4, CHUNKS)),
                 dma((2, 2, PEERS)),
                 dma((2, 2, PEERS)),
+                dma((2, PEERS)),
+                dma((2, PEERS)),
                 dma((2, 2, 8)),
                 dma((2, 2, 8)),
                 dma((2, 2, zs)),

time: 54.3 us -> 54.7 us (level)
  no operation moved by 1% of the time
where the time goes in v6:
time: 54.7 us; the launch traced here: 54.6 us
  Pallas kernels  52.8 us (97%)
  local copies, waits for them, and re-layouts  1.78 us (3%)
    pallas_call x1, Pallas kernels, body(): pl.pallas_call(functools.partial(body_kernel, (xs, zs, ch, chp, nr)), out...  52.8 us
    unnamed x1, local copies, waits for them, and re-layouts  1.78 us

profile of v6, /device:TPU:1, one launch (start us, length us, event | category | flops | bytes accessed | tf_op | source)
XLA Modules:
  0.0 54.6 jit_solution(10437124416156474959)
XLA Ops:
  0.0 52.8 %shard_map.82 = bf16[1,50,32,128]{3,2,1,0:T(8,128)(2,1)} custom-call(bf16[1,50,32,128]{3,2,1,0:T(8,128)(2,1)} %state_at.1, bf16[9,50,200]{2,1,0:T(8,128)(2,1)} %bitcast.4, f32[1,50]{1,0:T(1,128)} %bitcast.6, bf16[9,50,200]{2,1,0:T(8,128)(2,1)} %bitcast.5, f32[1,50]{1,0:T(1,128)} %bitcast.7, s32[1,32,128]{2,1,0:T(8,128)} %wet_at.1, s32[1,8]{1,0:T(1,128)} %nb_at.1, ...), custom_call_target="tpu_custom_call" | custom-call | tf_op jit(solution)/shard_map/pallas_call | solution.py:568
  52.8 1.8 %copy.10 = bf16[1,50,32,128]{3,2,1,0:T(8,128)(2,1)} copy(bf16[1,50,32,128]{3,2,1,0:T(8,128)(2,1)} %shard_map.82) | data formatting | bytes 819200

commit v7 on v6

--- a/solution.py
+++ b/solution.py
@@ -453,31 +453,55 @@
             for o in range(1, PEERS):
                 h_copy(layer, o, p).start()
 
-        near(0)
-        near(1)
-        far(0)
-        gather(layer, 0)
-        far(1)
-        along_x(0)
-        gather(layer, 1)
-        along_x(1)
-        gather(layer, 2)
-        along_y(0)
-        gather(layer, 3)
-        along_y(1)
-        if layer == 1:
+        def fixes():
             for p in range(2):
                 for o in range(1, PEERS):
                     f_copy(o, p).wait_recv()
             for j in range(PEERS):
                 fix_f[j, 0:ch, :] = fix[j, 2].astype(f32)
-        conv_chunk(layer, 0, 1, rows_of - 2)
-        for q in range(1, CHUNKS):
-            conv_chunk(layer, q, q * rows_of - 1, rows_of)
-            if layer == 0:
+
+        def conv(q):
+            if q == 0:
+                conv_chunk(layer, 0, 1, rows_of - 2)
+            else:
+                conv_chunk(layer, q, q * rows_of - 1, rows_of)
+
+        if layer == 0:
+            near(0)
+            near(1)
+            far(0)
+            gather(layer, 0)
+            far(1)
+            along_x(0)
+            gather(layer, 1)
+            along_x(1)
+            gather(layer, 2)
+            along_y(0)
+            gather(layer, 3)
+            along_y(1)
+            conv(0)
+            for q in range(1, CHUNKS):
+                conv(q)
                 hidden_inside(q - 1)
-        if layer == 0:
             hidden_inside(CHUNKS - 1)
+        else:
+            gather(layer, 0)
+            near(0)
+            gather(layer, 1)
+            near(1)
+            far(0)
+            gather(layer, 2)
+            far(1)
+            along_x(0)
+            fixes()
+            along_x(1)
+            gather(layer, 3)
+            conv(0)
+            conv(1)
+            along_y(0)
+            along_y(1)
+            conv(2)
+            conv(3)
         for p in range(2):
             for o in range(1, PEERS):
                 h_copy(layer, o, p).wait_recv()

time: 54.7 us -> 53.7 us (0.982)
  Pallas kernels: 52.8 us -> 51.8 us
    pallas_call x1, Pallas kernels: 52.8 us -> 51.8 us  [body(): pl.pallas_call(functools.partial(body_kernel, (xs, zs, ch, chp, nr)), out...]
where the time goes in v7:
time: 53.7 us; the launch traced here: 53.6 us
  Pallas kernels  51.8 us (96%)
  local copies, waits for them, and re-layouts  1.78 us (3%)
    pallas_call x1, Pallas kernels, body(): pl.pallas_call(functools.partial(body_kernel, (xs, zs, ch, chp, nr)), out...  51.8 us
    unnamed x1, local copies, waits for them, and re-layouts  1.78 us

profile of v7, /device:TPU:1, one launch (start us, length us, event | category | flops | bytes accessed | tf_op | source)
XLA Modules:
  0.0 53.6 jit_solution(7738533567853350951)
XLA Ops:
  0.0 51.8 %shard_map.82 = bf16[1,50,32,128]{3,2,1,0:T(8,128)(2,1)} custom-call(bf16[1,50,32,128]{3,2,1,0:T(8,128)(2,1)} %state_at.1, bf16[9,50,200]{2,1,0:T(8,128)(2,1)} %bitcast.4, f32[1,50]{1,0:T(1,128)} %bitcast.6, bf16[9,50,200]{2,1,0:T(8,128)(2,1)} %bitcast.5, f32[1,50]{1,0:T(1,128)} %bitcast.7, s32[1,32,128]{2,1,0:T(8,128)} %wet_at.1, s32[1,8]{1,0:T(1,128)} %nb_at.1, ...), custom_call_target="tpu_custom_call" | custom-call | tf_op jit(solution)/shard_map/pallas_call | solution.py:592
  51.8 1.8 %copy.10 = bf16[1,50,32,128]{3,2,1,0:T(8,128)(2,1)} copy(bf16[1,50,32,128]{3,2,1,0:T(8,128)(2,1)} %shard_map.82) | data formatting | bytes 819200

commit v8 on v7

--- a/solution.py
+++ b/solution.py
@@ -58,6 +58,7 @@
     fix_f,
     mask_cols,
     sums_cols,
+    result,
     table_own,
     table,
     table_s,
@@ -556,9 +557,19 @@
                 below = this
         return carry
 
-    lax.fori_loop(0, CHUNKS, final_chunk, 0)
-    out[0] = flat[0 : ch * nr].reshape(ch, nr, LANES).astype(bf16)
-
+    results = []
+    for part_of in range(2):
+        lax.fori_loop(part_of * CHUNKS // 2, (part_of + 1) * CHUNKS // 2, final_chunk, 0)
+        low = part_of * nr // 2
+        result[:, low : low + nr // 2, :] = flat[0 : ch * nr].reshape(ch, nr, LANES)[:, low : low + nr // 2].astype(bf16)
+        rows = pl.ds(low, nr // 2)
+        results.append(
+            pltpu.make_async_copy(result.at[:, rows, :], out.at[0, :, rows, :], local_sem.at[9 + part_of])
+        )
+        results[-1].start()
+
+    for copy in results:
+        copy.wait()
     for o in range(1, xs):
         t_copy(o).wait_send()
     for p in range(2):
@@ -588,12 +599,11 @@
         pairs = nr // 2
         f32, bf16 = jnp.float32, jnp.bfloat16
         vmem, dma = pltpu.VMEM, pltpu.SemaphoreType.DMA
-        inside = pl.BlockSpec(memory_space=pltpu.VMEM)
         return pl.pallas_call(
             functools.partial(body_kernel, (xs, zs, ch, chp, nr)),
             out_shape=jax.ShapeDtypeStruct(state.shape, bf16),
             in_specs=[pl.BlockSpec(memory_space=pl.ANY)] * 8,
-            out_specs=inside,
+            out_specs=pl.BlockSpec(memory_space=pl.ANY),
             scratch_shapes=[
                 vmem(state.shape, bf16),
                 vmem((9, ch, PEERS * ch), bf16),
@@ -625,6 +635,7 @@
                 vmem((PEERS, chp, LANES), f32),
                 vmem((8, LANES), f32),
                 vmem((chp, LANES), f32),
+                vmem((ch, nr, LANES), bf16),
                 vmem((8, LANES), jnp.int32),
                 vmem((xs, 8, LANES), jnp.int32),
                 pltpu.SMEM((xs, 8, LANES), jnp.int32),
@@ -642,7 +653,7 @@
                 dma((2, 2, xs)),
                 dma((xs,)),
                 dma((xs,)),
-                dma((9,)),
+                dma((11,)),
             ],
             compiler_params=pltpu.CompilerParams(
                 collective_id=0, has_side_effects=True, vmem_limit_bytes=63 * 1024 * 1024

time: 53.7 us -> 53.7 us (level)
  no operation moved by 1% of the time
where the time goes in v8:
time: 53.7 us; the launch traced here: 53.5 us
  Pallas kernels  51.8 us (96%)
  local copies, waits for them, and re-layouts  1.78 us (3%)
    pallas_call x1, Pallas kernels, body(): pl.pallas_call(functools.partial(body_kernel, (xs, zs, ch, chp, nr)), out...  51.8 us
    unnamed x1, local copies, waits for them, and re-layouts  1.78 us

profile of v8, /device:TPU:1, one launch (start us, length us, event | category | flops | bytes accessed | tf_op | source)
XLA Modules:
  0.0 53.5 jit_solution(11553944209141093427)
XLA Ops:
  0.0 51.8 %shard_map.82 = bf16[1,50,32,128]{3,2,1,0:T(8,128)(2,1)} custom-call(bf16[1,50,32,128]{3,2,1,0:T(8,128)(2,1)} %state_at.1, bf16[9,50,200]{2,1,0:T(8,128)(2,1)} %bitcast.4, f32[1,50]{1,0:T(1,128)} %bitcast.6, bf16[9,50,200]{2,1,0:T(8,128)(2,1)} %bitcast.5, f32[1,50]{1,0:T(1,128)} %bitcast.7, s32[1,32,128]{2,1,0:T(8,128)} %wet_at.1, s32[1,8]{1,0:T(1,128)} %nb_at.1, ...), custom_call_target="tpu_custom_call" | custom-call | tf_op jit(solution)/shard_map/pallas_call | solution.py:602
  51.8 1.8 %copy.10 = bf16[1,50,32,128]{3,2,1,0:T(8,128)(2,1)} copy(bf16[1,50,32,128]{3,2,1,0:T(8,128)(2,1)} %shard_map.82) | data formatting | bytes 819200

commit v9 on v8

--- a/solution.py
+++ b/solution.py
@@ -443,7 +443,7 @@
                 return carry
 
             lax.fori_loop(0, xs, one_slot, 0)
-            for o in range(1, xs):
+            for o in (2, 1, 3):
                 u_copy(layer, o, p).start()
             slots_x[layer][p][x] = slots[p][layer, x]
 
@@ -451,7 +451,7 @@
             for o in range(1, xs):
                 u_copy(layer, o, p).wait_recv()
             (merge_rows, merge_cols)[p](layer)
-            for o in range(1, PEERS):
+            for o in (2, 1, 3):
                 h_copy(layer, o, p).start()
 
         def fixes():

time: 53.7 us -> 53.5 us (level)
  no operation moved by 1% of the time
where the time goes in v9:
time: 53.5 us; the launch traced here: 53.4 us
  Pallas kernels  51.6 us (96%)
  local copies, waits for them, and re-layouts  1.78 us (3%)
    pallas_call x1, Pallas kernels, body(): pl.pallas_call(functools.partial(body_kernel, (xs, zs, ch, chp, nr)), out...  51.6 us
    unnamed x1, local copies, waits for them, and re-layouts  1.78 us

profile of v9, /device:TPU:1, one launch (start us, length us, event | category | flops | bytes accessed | tf_op | source)
XLA Modules:
  0.0 53.4 jit_solution(212488573080920642)
XLA Ops:
  0.0 51.6 %shard_map.82 = bf16[1,50,32,128]{3,2,1,0:T(8,128)(2,1)} custom-call(bf16[1,50,32,128]{3,2,1,0:T(8,128)(2,1)} %state_at.1, bf16[9,50,200]{2,1,0:T(8,128)(2,1)} %bitcast.4, f32[1,50]{1,0:T(1,128)} %bitcast.6, bf16[9,50,200]{2,1,0:T(8,128)(2,1)} %bitcast.5, f32[1,50]{1,0:T(1,128)} %bitcast.7, s32[1,32,128]{2,1,0:T(8,128)} %wet_at.1, s32[1,8]{1,0:T(1,128)} %nb_at.1, ...), custom_call_target="tpu_custom_call" | custom-call | tf_op jit(solution)/shard_map/pallas_call | solution.py:602
  51.6 1.8 %copy.10 = bf16[1,50,32,128]{3,2,1,0:T(8,128)(2,1)} copy(bf16[1,50,32,128]{3,2,1,0:T(8,128)(2,1)} %shard_map.82) | data formatting | bytes 819200
